TPU v7x, 32 devices: a whole 2x2x4 slice. The times are simulated.
32 devices in a mesh: dp: 8 (over z, x), grp: 4 (over y, core).
Axes of the slice: x: 2, y: 2, z: 4, core: 2. Of those that a mesh axis runs over, the one named last changes fastest.
Arguments:
- tokens: bfloat16 [8192, 1024], P(('dp', 'grp')), may hold values from -6 to 6
- memory: bfloat16 [2048, 1024], P(('dp', 'grp')), may hold values from -6 to 6
- cotangent: bfloat16 [8192, 1024], P(('dp', 'grp')), may hold values from -6 to 6
- bucket: int32 [8], P('dp'), may hold values from 0 to 2
- gain_self: bfloat16 [1024], replicated, may hold values from 0.099609375 to 1.8984375
- self_query: bfloat16 [1024, 1024], replicated, may hold values from -0.046875 to 0.046875
- self_key: bfloat16 [1024, 512], replicated, may hold values from -0.1875 to 0.1875
- self_value: bfloat16 [1024, 512], replicated, may hold values from -0.1875 to 0.1875
- self_out: bfloat16 [1024, 1024], replicated, may hold values from -0.75 to 0.75
- rel_bias: bfloat16 [32, 16], replicated, may hold values from -5 to 5
- gain_cross: bfloat16 [1024], replicated, may hold values from 0.099609375 to 1.8984375
- cross_query: bfloat16 [1024, 1024], replicated, may hold values from -0.046875 to 0.046875
- cross_key: bfloat16 [1024, 512], replicated, may hold values from -0.1875 to 0.1875
- cross_value: bfloat16 [1024, 512], replicated, may hold values from -0.1875 to 0.1875
- cross_out: bfloat16 [1024, 1024], replicated, may hold values from -0.75 to 0.75
- gain_ffn: bfloat16 [1024], replicated, may hold values from 0.099609375 to 1.8984375
- ffn_gate: bfloat16 [1024, 2816], replicated, may hold values from -0.1875 to 0.1875
- ffn_up: bfloat16 [1024, 2816], replicated, may hold values from -0.1875 to 0.1875
- ffn_down: bfloat16 [2816, 1024], replicated, may hold values from -0.109375 to 0.109375
Outputs:
- layer_out: bfloat16 [8192, 1024], P(('dp', 'grp'))
- grad_tokens: bfloat16 [8192, 1024], P(('dp', 'grp'))
- grad_memory: bfloat16 [2048, 1024], P(('dp', 'grp'))
- grad_gain_self: float32 [1024], P(('dp', 'grp'))
- grad_self_query: float32 [1024, 1024], P(('dp', 'grp'))
- grad_self_key: float32 [1024, 512], P(('dp', 'grp'))
- grad_self_value: float32 [1024, 512], P(('dp', 'grp'))
- grad_self_out: float32 [1024, 1024], P(('dp', 'grp'))
- grad_rel_bias: float32 [512], P(('dp', 'grp'))
- grad_gain_cross: float32 [1024], P(('dp', 'grp'))
- grad_cross_query: float32 [1024, 1024], P(('dp', 'grp'))
- grad_cross_key: float32 [1024, 512], P(('dp', 'grp'))
- grad_cross_value: float32 [1024, 512], P(('dp', 'grp'))
- grad_cross_out: float32 [1024, 1024], P(('dp', 'grp'))
- grad_gain_ffn: float32 [1024], P(('dp', 'grp'))
- grad_ffn_gate: float32 [1024, 2816], P(('dp', 'grp'))
- grad_ffn_up: float32 [1024, 2816], P(('dp', 'grp'))
- grad_ffn_down: float32 [2816, 1024], P(('dp', 'grp'))
All inputs are finite; a program needn't handle non-finite values.
Results may differ from a plain program's by a relative error of at most 0.04.
Values may be sent and summed in bfloat16 or wider, within the bound.
No kernel may reach another device: no remote copies, remote signals or barrier semaphores. Data moves between devices by JAX's collectives and lax.ppermute only.
A program may use at most 256 MiB of HBM per device.

v0:
```python
import jax
import jax.numpy as jnp
from jax import lax
from jax.sharding import PartitionSpec as P

HEADS = 16
HEAD = 64
BUCKETS = 32
SHORT = 1024
RATIO = 4
BLOCK = 512


EPSILON = 1e-06
NEGATIVE = -1e30
THRESHOLDS = (19, 21, 24, 27, 31, 35, 40, 46, 52, 59, 67, 77, 87, 99, 113)


def rel_bucket(distance):
    distance = jnp.maximum(distance, 0)
    beyond = 16 + sum(((distance >= border).astype(jnp.int32) for border in THRESHOLDS))
    return jnp.where(distance < 16, distance, beyond)


def doc_length(bucket_id, group_rows):
    halved = jnp.right_shift(jnp.int32(group_rows), bucket_id)
    return jnp.minimum(group_rows, jnp.maximum(SHORT, halved))


def norm_apply(hidden, gain_vec):
    return (
        hidden * lax.rsqrt(jnp.mean(hidden * hidden, axis=-1, keepdims=True) + EPSILON) * gain_vec
    )


def gated_unit(gate_val, up_val):
    return jax.nn.gelu(gate_val, approximate=True) * up_val


def matmul(left_op, right_op):
    return jnp.dot(left_op, right_op, preferred_element_type=jnp.float32)


def matmul_left(left_op, right_op):
    return lax.dot_general(
        left_op, right_op, (((0,), (0,)), ((), ())), preferred_element_type=jnp.float32
    )


def matmul_right(left_op, right_op):
    return lax.dot_general(
        left_op, right_op, (((1,), (1,)), ((), ())), preferred_element_type=jnp.float32
    )


def take_block(stacked, number):
    return lax.dynamic_index_in_dim(stacked, number, 0, keepdims=False)


def add_block(stacked, number, update):
    return lax.dynamic_update_index_in_dim(stacked, take_block(stacked, number) + update, number, 0)


def near_tables(rel_local):
    near_count = (111 + 2 * BLOCK) // BLOCK
    inside = jnp.arange(BLOCK, dtype=jnp.int32)
    bucket_ids = jnp.arange(BUCKETS, dtype=jnp.int32)
    tables = []
    for offset in range(near_count):
        distance = offset * BLOCK + inside[:, None] - inside[None, :]
        tables.append((rel_bucket(distance)[:, :, None] == bucket_ids).astype(jnp.bfloat16))
    onehot = jnp.stack(tables)
    biases = jnp.einsum("oacb,bh->ohac", onehot, rel_local, preferred_element_type=jnp.float32)
    return (onehot, biases)


def self_scores(q_block, key_blocks, bias_near, rel_local, q_index, k_index):
    k_block = take_block(key_blocks, k_index)
    scores = jnp.einsum("akrd,ckd->krac", q_block, k_block, preferred_element_type=jnp.float32)
    offset = q_index - k_index
    near_count = bias_near.shape[0]
    heads_local = scores.shape[0] * scores.shape[1]

    def near_term():
        return take_block(bias_near, jnp.minimum(offset, near_count - 1))

    def far_term():
        return jnp.broadcast_to(
            rel_local[BUCKETS - 1].astype(jnp.float32)[:, None, None], (heads_local, BLOCK, BLOCK)
        )

    shift_term = lax.cond(offset < near_count, near_term, far_term)
    scores = scores + shift_term.reshape(scores.shape)
    inside = jnp.arange(BLOCK, dtype=jnp.int32)
    allowed = offset * BLOCK + inside[:, None] - inside[None, :] >= 0
    return jnp.where(allowed, scores, NEGATIVE)


def split_heads(q_heads, k_heads):
    group_rows = q_heads.shape[0]
    kv_local = k_heads.shape[1] // HEAD
    group_ratio = q_heads.shape[1] // k_heads.shape[1]
    return (group_rows, kv_local, group_ratio, group_rows // BLOCK)


def rows_first(stat):
    return jnp.moveaxis(stat, -1, 0)[..., None]


def self_forward(q_heads, k_heads, v_heads, bias_near, rel_local, length):
    group_rows, kv_local, group_ratio, blocks = split_heads(q_heads, k_heads)
    queries = q_heads.reshape(blocks, BLOCK, kv_local, group_ratio, HEAD)
    key_blocks = k_heads.reshape(blocks, BLOCK, kv_local, HEAD)
    value_blocks = v_heads.reshape(blocks, BLOCK, kv_local, HEAD)

    def one_block(q_index):
        q_block = take_block(queries, q_index)
        first_block = q_index * BLOCK // length * length // BLOCK

        def value_pass(k_index, running):
            row_peak, summed, accumulated = running
            scores = self_scores(q_block, key_blocks, bias_near, rel_local, q_index, k_index)
            new_peak = jnp.maximum(row_peak, jnp.max(scores, axis=-1))
            rescale = jnp.exp(row_peak - new_peak)
            weights = jnp.exp(scores - new_peak[..., None])
            summed = summed * rescale + jnp.sum(weights, axis=-1)
            accumulated = accumulated * rows_first(rescale) + jnp.einsum(
                "krac,ckd->akrd",
                weights.astype(jnp.bfloat16),
                take_block(value_blocks, k_index),
                preferred_element_type=jnp.float32,
            )
            return (new_peak, summed, accumulated)

        start_state = (
            jnp.full((kv_local, group_ratio, BLOCK), NEGATIVE, jnp.float32),
            jnp.zeros((kv_local, group_ratio, BLOCK), jnp.float32),
            jnp.zeros((BLOCK, kv_local, group_ratio, HEAD), jnp.float32),
        )
        row_peak, summed, accumulated = lax.fori_loop(
            first_block, q_index + 1, value_pass, start_state
        )
        return (accumulated / rows_first(summed), row_peak + jnp.log(summed))

    attended, log_total = lax.map(one_block, jnp.arange(blocks, dtype=jnp.int32))
    return (attended.reshape(group_rows, kv_local * group_ratio * HEAD), log_total)


def self_backward(
    q_heads, k_heads, v_heads, grad_heads, attended, log_total, onehot, bias_near, rel_local, length
):
    group_rows, kv_local, group_ratio, blocks = split_heads(q_heads, k_heads)
    heads_local = kv_local * group_ratio
    near_count = onehot.shape[0]
    queries = q_heads.reshape(blocks, BLOCK, kv_local, group_ratio, HEAD)
    grad_blocks = grad_heads.reshape(blocks, BLOCK, kv_local, group_ratio, HEAD)
    out_blocks = attended.reshape(blocks, BLOCK, kv_local, group_ratio, HEAD)
    key_blocks = k_heads.reshape(blocks, BLOCK, kv_local, HEAD)
    value_blocks = v_heads.reshape(blocks, BLOCK, kv_local, HEAD)

    def one_block(running, q_index):
        q_block = take_block(queries, q_index)
        g_block = take_block(grad_blocks, q_index)
        lse_block = take_block(log_total, q_index)
        first_block = q_index * BLOCK // length * length // BLOCK
        row_delta = jnp.moveaxis(
            jnp.sum(g_block.astype(jnp.float32) * take_block(out_blocks, q_index), axis=-1), 0, -1
        )

        def grad_pass(k_index, inner_state):
            d_query, d_keys, d_values, d_bias = inner_state
            k_block = take_block(key_blocks, k_index)
            v_block = take_block(value_blocks, k_index)
            scores = self_scores(q_block, key_blocks, bias_near, rel_local, q_index, k_index)
            prob_full = jnp.exp(scores - lse_block[..., None])
            d_probs = jnp.einsum(
                "akrd,ckd->krac", g_block, v_block, preferred_element_type=jnp.float32
            )
            d_scores = (prob_full * (d_probs - row_delta[..., None])).astype(jnp.bfloat16)
            d_query = d_query + jnp.einsum(
                "krac,ckd->akrd", d_scores, k_block, preferred_element_type=jnp.float32
            )
            d_keys = add_block(
                d_keys,
                k_index,
                jnp.einsum("krac,akrd->ckd", d_scores, q_block, preferred_element_type=jnp.float32),
            )
            d_values = add_block(
                d_values,
                k_index,
                jnp.einsum(
                    "krac,akrd->ckd",
                    prob_full.astype(jnp.bfloat16),
                    g_block,
                    preferred_element_type=jnp.float32,
                ),
            )
            offset = q_index - k_index
            flat_scores = d_scores.reshape(heads_local, BLOCK, BLOCK)

            def near_grad():
                return jnp.einsum(
                    "hac,acb->bh",
                    flat_scores,
                    take_block(onehot, jnp.minimum(offset, near_count - 1)),
                    preferred_element_type=jnp.float32,
                )

            def far_grad():
                return (
                    jnp.zeros((BUCKETS, heads_local), jnp.float32)
                    .at[BUCKETS - 1]
                    .set(jnp.sum(flat_scores.astype(jnp.float32), axis=(1, 2)))
                )

            d_bias = d_bias + lax.cond(offset < near_count, near_grad, far_grad)
            return (d_query, d_keys, d_values, d_bias)

        d_keys, d_values, d_bias = running
        start_state = (
            jnp.zeros((BLOCK, kv_local, group_ratio, HEAD), jnp.float32),
            d_keys,
            d_values,
            d_bias,
        )
        d_query, d_keys, d_values, d_bias = lax.fori_loop(
            first_block, q_index + 1, grad_pass, start_state
        )
        return ((d_keys, d_values, d_bias), d_query)

    start_carry = (
        jnp.zeros((blocks, BLOCK, kv_local, HEAD), jnp.float32),
        jnp.zeros((blocks, BLOCK, kv_local, HEAD), jnp.float32),
        jnp.zeros((BUCKETS, heads_local), jnp.float32),
    )
    (d_keys, d_values, d_bias), d_query = lax.scan(
        one_block, start_carry, jnp.arange(blocks, dtype=jnp.int32)
    )
    return (
        d_query.reshape(group_rows, heads_local * HEAD),
        d_keys.reshape(group_rows, kv_local * HEAD),
        d_values.reshape(group_rows, kv_local * HEAD),
        d_bias,
    )


def cross_scores(q_block, mem_keys, q_index, length, mem_length):
    scores = jnp.einsum("akrd,ckd->krac", q_block, mem_keys, preferred_element_type=jnp.float32)
    q_docs = (q_index * BLOCK + jnp.arange(BLOCK, dtype=jnp.int32)) // length
    m_docs = jnp.arange(mem_keys.shape[0], dtype=jnp.int32) // mem_length
    return jnp.where(q_docs[:, None] == m_docs[None, :], scores, NEGATIVE)


def cross_forward(q_heads, km_heads, vm_heads, length, mem_length):
    group_rows, kv_local, group_ratio, blocks = split_heads(q_heads, km_heads)
    queries = q_heads.reshape(blocks, BLOCK, kv_local, group_ratio, HEAD)
    mem_keys = km_heads.reshape(km_heads.shape[0], kv_local, HEAD)
    mem_values = vm_heads.reshape(vm_heads.shape[0], kv_local, HEAD)

    def one_block(q_index):
        scores = cross_scores(take_block(queries, q_index), mem_keys, q_index, length, mem_length)
        prob_low = jax.nn.softmax(scores, axis=-1).astype(jnp.bfloat16)
        return jnp.einsum(
            "krac,ckd->akrd", prob_low, mem_values, preferred_element_type=jnp.float32
        )

    attended = lax.map(one_block, jnp.arange(blocks, dtype=jnp.int32))
    return attended.reshape(group_rows, kv_local * group_ratio * HEAD)


def cross_backward(q_heads, km_heads, vm_heads, grad_heads, length, mem_length):
    group_rows, kv_local, group_ratio, blocks = split_heads(q_heads, km_heads)
    queries = q_heads.reshape(blocks, BLOCK, kv_local, group_ratio, HEAD)
    grad_blocks = grad_heads.reshape(blocks, BLOCK, kv_local, group_ratio, HEAD)
    mem_keys = km_heads.reshape(km_heads.shape[0], kv_local, HEAD)
    mem_values = vm_heads.reshape(vm_heads.shape[0], kv_local, HEAD)

    def one_block(running, q_index):
        d_keys, d_values = running
        q_block = take_block(queries, q_index)
        g_block = take_block(grad_blocks, q_index)
        prob_full = jax.nn.softmax(
            cross_scores(q_block, mem_keys, q_index, length, mem_length), axis=-1
        )
        d_probs = jnp.einsum(
            "akrd,ckd->krac", g_block, mem_values, preferred_element_type=jnp.float32
        )
        row_delta = jnp.sum(prob_full * d_probs, axis=-1, keepdims=True)
        d_scores = (prob_full * (d_probs - row_delta)).astype(jnp.bfloat16)
        d_query = jnp.einsum(
            "krac,ckd->akrd", d_scores, mem_keys, preferred_element_type=jnp.float32
        )
        d_keys = d_keys + jnp.einsum(
            "krac,akrd->ckd", d_scores, q_block, preferred_element_type=jnp.float32
        )
        d_values = d_values + jnp.einsum(
            "krac,akrd->ckd",
            prob_full.astype(jnp.bfloat16),
            g_block,
            preferred_element_type=jnp.float32,
        )
        return ((d_keys, d_values), d_query)

    start_carry = (jnp.zeros(mem_keys.shape, jnp.float32), jnp.zeros(mem_values.shape, jnp.float32))
    (d_keys, d_values), d_query = lax.scan(
        one_block, start_carry, jnp.arange(blocks, dtype=jnp.int32)
    )
    return (
        d_query.reshape(group_rows, kv_local * group_ratio * HEAD),
        d_keys.reshape(km_heads.shape),
        d_values.reshape(vm_heads.shape),
    )


def shards(
    tokens,
    memory,
    cotangent,
    bucket,
    gain_self,
    self_query,
    self_key,
    self_value,
    self_out,
    rel_bias,
    gain_cross,
    cross_query,
    cross_key,
    cross_value,
    cross_out,
    gain_ffn,
    ffn_gate,
    ffn_up,
    ffn_down,
):
    groups = lax.axis_size("grp")
    heads_local = HEADS // groups
    group_rows = tokens.shape[0] * groups
    length = doc_length(bucket[0], group_rows)
    mem_length = length // RATIO
    head_start = lax.axis_index("grp") * heads_local
    rel_local = lax.dynamic_slice_in_dim(rel_bias, head_start, heads_local, 1)
    onehot, bias_near = near_tables(rel_local)
    hidden_in = tokens.astype(jnp.float32)
    normed_one, norm_back_one = jax.vjp(norm_apply, hidden_in, gain_self.astype(jnp.float32))
    low_one = normed_one.astype(jnp.bfloat16)
    query_rows = matmul(low_one, self_query).astype(jnp.bfloat16)
    key_rows = matmul(low_one, self_key).astype(jnp.bfloat16)
    value_rows = matmul(low_one, self_value).astype(jnp.bfloat16)
    key_mem = matmul(memory, cross_key).astype(jnp.bfloat16)
    value_mem = matmul(memory, cross_value).astype(jnp.bfloat16)
    q_heads, k_heads, v_heads, km_heads, vm_heads = (
        lax.all_to_all(query_rows, "grp", split_axis=1, concat_axis=0, tiled=True),
        lax.all_to_all(key_rows, "grp", split_axis=1, concat_axis=0, tiled=True),
        lax.all_to_all(value_rows, "grp", split_axis=1, concat_axis=0, tiled=True),
        lax.all_to_all(key_mem, "grp", split_axis=1, concat_axis=0, tiled=True),
        lax.all_to_all(value_mem, "grp", split_axis=1, concat_axis=0, tiled=True),
    )
    attended, log_total = self_forward(q_heads, k_heads, v_heads, bias_near, rel_local, length)
    attended_rows = lax.all_to_all(
        attended.astype(jnp.bfloat16), "grp", split_axis=0, concat_axis=1, tiled=True
    )
    hidden_mid = hidden_in + matmul(attended_rows, self_out)
    normed_two, norm_back_two = jax.vjp(norm_apply, hidden_mid, gain_cross.astype(jnp.float32))
    low_two = normed_two.astype(jnp.bfloat16)
    cq_heads = lax.all_to_all(
        matmul(low_two, cross_query).astype(jnp.bfloat16),
        "grp",
        split_axis=1,
        concat_axis=0,
        tiled=True,
    )
    crossed = cross_forward(cq_heads, km_heads, vm_heads, length, mem_length).astype(jnp.bfloat16)
    crossed_rows = lax.all_to_all(crossed, "grp", split_axis=0, concat_axis=1, tiled=True)
    hidden_late = hidden_mid + matmul(crossed_rows, cross_out)
    normed_three, norm_back_three = jax.vjp(norm_apply, hidden_late, gain_ffn.astype(jnp.float32))
    low_three = normed_three.astype(jnp.bfloat16)
    gate_pre = matmul(low_three, ffn_gate)
    up_pre = matmul(low_three, ffn_up)
    inner_act, gated_back = jax.vjp(gated_unit, gate_pre, up_pre)
    inner_low = inner_act.astype(jnp.bfloat16)
    layer_out = (hidden_late + matmul(inner_low, ffn_down)).astype(jnp.bfloat16)
    d_ffn_down = matmul_left(inner_low, cotangent)
    d_inner = matmul_right(cotangent, ffn_down).astype(jnp.bfloat16).astype(jnp.float32)
    d_gate, d_up = gated_back(d_inner)
    d_gate_low = d_gate.astype(jnp.bfloat16)
    d_up_low = d_up.astype(jnp.bfloat16)
    d_ffn_gate = matmul_left(low_three, d_gate_low)
    d_ffn_up = matmul_left(low_three, d_up_low)
    d_late_norm, d_gain_ffn = norm_back_three(
        matmul_right(d_gate_low, ffn_gate) + matmul_right(d_up_low, ffn_up)
    )
    grad_late = cotangent.astype(jnp.float32) + d_late_norm
    late_low = grad_late.astype(jnp.bfloat16)
    d_cross_out = matmul_left(crossed_rows, late_low)
    d_crossed_heads = lax.all_to_all(
        matmul_right(late_low, cross_out).astype(jnp.bfloat16),
        "grp",
        split_axis=1,
        concat_axis=0,
        tiled=True,
    )
    dq_cross, dk_cross, dv_cross = cross_backward(
        cq_heads, km_heads, vm_heads, d_crossed_heads, length, mem_length
    )
    dq_rows, dk_rows, dv_rows = (
        lax.all_to_all(
            dq_cross.astype(jnp.bfloat16), "grp", split_axis=0, concat_axis=1, tiled=True
        ),
        lax.all_to_all(
            dk_cross.astype(jnp.bfloat16), "grp", split_axis=0, concat_axis=1, tiled=True
        ),
        lax.all_to_all(
            dv_cross.astype(jnp.bfloat16), "grp", split_axis=0, concat_axis=1, tiled=True
        ),
    )
    d_cross_query = matmul_left(low_two, dq_rows)
    d_cross_key = matmul_left(memory, dk_rows)
    d_cross_value = matmul_left(memory, dv_rows)
    grad_memory = (matmul_right(dk_rows, cross_key) + matmul_right(dv_rows, cross_value)).astype(
        jnp.bfloat16
    )
    d_mid_norm, d_gain_cross = norm_back_two(matmul_right(dq_rows, cross_query))
    grad_mid = grad_late + d_mid_norm
    mid_low = grad_mid.astype(jnp.bfloat16)
    d_self_out = matmul_left(attended_rows, mid_low)
    d_attended_heads = lax.all_to_all(
        matmul_right(mid_low, self_out).astype(jnp.bfloat16),
        "grp",
        split_axis=1,
        concat_axis=0,
        tiled=True,
    )
    dq_self, dk_self, dv_self, d_bias_local = self_backward(
        q_heads,
        k_heads,
        v_heads,
        d_attended_heads,
        attended,
        log_total,
        onehot,
        bias_near,
        rel_local,
        length,
    )
    dq_back, dk_back, dv_back = (
        lax.all_to_all(
            dq_self.astype(jnp.bfloat16), "grp", split_axis=0, concat_axis=1, tiled=True
        ),
        lax.all_to_all(
            dk_self.astype(jnp.bfloat16), "grp", split_axis=0, concat_axis=1, tiled=True
        ),
        lax.all_to_all(
            dv_self.astype(jnp.bfloat16), "grp", split_axis=0, concat_axis=1, tiled=True
        ),
    )
    d_self_query = matmul_left(low_one, dq_back)
    d_self_key = matmul_left(low_one, dk_back)
    d_self_value = matmul_left(low_one, dv_back)
    d_in_norm, d_gain_self = norm_back_one(
        matmul_right(dq_back, self_query)
        + matmul_right(dk_back, self_key)
        + matmul_right(dv_back, self_value)
    )
    grad_tokens = (grad_mid + d_in_norm).astype(jnp.bfloat16)
    d_rel_bias = lax.dynamic_update_slice(
        jnp.zeros((BUCKETS, HEADS), jnp.float32), d_bias_local, (jnp.int32(0), head_start)
    ).reshape(BUCKETS * HEADS)
    summed = (
        lax.psum_scatter(d_gain_self, ("dp", "grp"), scatter_dimension=0, tiled=True),
        lax.psum_scatter(d_self_query, ("dp", "grp"), scatter_dimension=0, tiled=True),
        lax.psum_scatter(d_self_key, ("dp", "grp"), scatter_dimension=0, tiled=True),
        lax.psum_scatter(d_self_value, ("dp", "grp"), scatter_dimension=0, tiled=True),
        lax.psum_scatter(d_self_out, ("dp", "grp"), scatter_dimension=0, tiled=True),
        lax.psum_scatter(d_rel_bias, ("dp", "grp"), scatter_dimension=0, tiled=True),
        lax.psum_scatter(d_gain_cross, ("dp", "grp"), scatter_dimension=0, tiled=True),
        lax.psum_scatter(d_cross_query, ("dp", "grp"), scatter_dimension=0, tiled=True),
        lax.psum_scatter(d_cross_key, ("dp", "grp"), scatter_dimension=0, tiled=True),
        lax.psum_scatter(d_cross_value, ("dp", "grp"), scatter_dimension=0, tiled=True),
        lax.psum_scatter(d_cross_out, ("dp", "grp"), scatter_dimension=0, tiled=True),
        lax.psum_scatter(d_gain_ffn, ("dp", "grp"), scatter_dimension=0, tiled=True),
        lax.psum_scatter(d_ffn_gate, ("dp", "grp"), scatter_dimension=0, tiled=True),
        lax.psum_scatter(d_ffn_up, ("dp", "grp"), scatter_dimension=0, tiled=True),
        lax.psum_scatter(d_ffn_down, ("dp", "grp"), scatter_dimension=0, tiled=True),
    )
    return (
        layer_out,
        grad_tokens,
        grad_memory,
        summed[0],
        summed[1],
        summed[2],
        summed[3],
        summed[4],
        summed[5],
        summed[6],
        summed[7],
        summed[8],
        summed[9],
        summed[10],
        summed[11],
        summed[12],
        summed[13],
        summed[14],
    )


def solution(mesh):
    in_specs = (
        P(("dp", "grp"), None),
        P(("dp", "grp"), None),
        P(("dp", "grp"), None),
        P("dp"),
        P(),
        P(),
        P(),
        P(),
        P(),
        P(),
        P(),
        P(),
        P(),
        P(),
        P(),
        P(),
        P(),
        P(),
        P(),
    )
    out_specs = (
        P(("dp", "grp"), None),
        P(("dp", "grp"), None),
        P(("dp", "grp"), None),
        P(("dp", "grp")),
        P(("dp", "grp"), None),
        P(("dp", "grp"), None),
        P(("dp", "grp"), None),
        P(("dp", "grp"), None),
        P(("dp", "grp")),
        P(("dp", "grp")),
        P(("dp", "grp"), None),
        P(("dp", "grp"), None),
        P(("dp", "grp"), None),
        P(("dp", "grp"), None),
        P(("dp", "grp")),
        P(("dp", "grp"), None),
        P(("dp", "grp"), None),
        P(("dp", "grp"), None),
    )
    return jax.shard_map(shards, mesh=mesh, in_specs=in_specs, out_specs=out_specs, check_vma=False)
```

profile of v0, /device:TPU:0, one launch (start us, length us, event | category | flops | bytes accessed | tf_op | source)
XLA Modules:
  0.0 1866.0 jit_solution(9549443061385386332)
XLA Ops:
  44.6 12.9 fusion.112
  71.2 60.9 %while.140 = (s32[]{:T(128)}, f32[2,512,2,2,64]{1,4,3,2,0:T(8,128)}, f32[2,2,2,512]{3,2,1,0:T(2,128)S(1)}, s32[2]{0:T(128)S(1)}, s32[]{:T(128)}, /*index=5*/s32[...) while((s32[]{:T(128)}, f32[2,512,2,2,64]{1,4,3,2,0:T(8,128)}, ...), condition=%wide.region_8.9_spmd.clone, body=%wide.region_1.8_spmd.sunk.clone | while | flops 276701728 | bytes 37934000 | solution.py:145
  76.1 16.4 while.139
  98.3 32.8 %while.139 = (s32[]{:T(128)}, f32[2,2,512]{2,1,0:T(2,128)S(1)}, f32[2,2,512]{2,1,0:T(2,128)S(1)}, f32[512,2,2,64]{0,3,2,1:T(8,128)S(1)}, s32[]{:T(128)}, /*index...) while((s32[]{:T(128)}, f32[2,2,512]{2,1,0:T(2,128)S(1)}, ...), condition=%wide.region_7.7_spmd, body=%wide.region_2.6_spmd.sunk | while | flops 276568576 | bytes 35787056 | solution.py:140
  180.6 11.9 while.141
  261.2 15.4 while.144
  323.7 16.0 fusion.111
  345.7 120.2 %while.143 = (s32[]{:T(128)}, f32[2,512,2,64]{1,3,2,0:T(8,128)}, f32[2,512,2,64]{1,3,2,0:T(8,128)}, f32[32,4]{0,1:T(4,128)S(1)}, bf16[2,512,2,2,64]{1,4,3,2,0:T(...) while((s32[]{:T(128)}, f32[2,512,2,64]{1,3,2,0:T(8,128)}, ...), condition=%wide.region_31.32_spmd.clone, body=%wide.region_22.31_spmd.sunk.clone | while | flops 746715776 | bytes 71482512 | solution.py:236
  351.9 35.4 %while.142 = (s32[]{:T(128)}, f32[512,2,2,64]{0,3,2,1:T(8,128)S(1)}, f32[2,512,2,64]{1,3,2,0:T(8,128)}, f32[2,512,2,64]{1,3,2,0:T(8,128)}, f32[32,4]{0,1:T(4,128...) while((s32[]{:T(128)}, f32[512,2,2,64]{0,3,2,1:T(8,128)S(1)}, ...), condition=%wide.region_30.30_spmd, body=%wide.region_24.29_spmd.sunk | while | flops 746324608 | bytes 68049344 | solution.py:226
  370.5 13.9 conditional.7
  394.3 70.9 %while.142 = (s32[]{:T(128)}, f32[512,2,2,64]{0,3,2,1:T(8,128)S(1)}, f32[2,512,2,64]{1,3,2,0:T(8,128)}, f32[2,512,2,64]{1,3,2,0:T(8,128)}, f32[32,4]{0,1:T(4,128...) while((s32[]{:T(128)}, f32[512,2,2,64]{0,3,2,1:T(8,128)S(1)}, ...), condition=%wide.region_30.30_spmd, body=%wide.region_24.29_spmd.sunk | while | flops 746324608 | bytes 68049344 | solution.py:226
  412.9 14.0 conditional.7
  448.4 13.9 conditional.7
  507.2 11.9 all_to_all.259
  561.0 42.0 %all-reduce.5 = (f32[1024]{0:T(1024)S(1)}, f32[512]{0:T(512)S(1)}, f32[1024]{0:T(1024)S(1)}, f32[1024]{0:T(1024)S(1)}) all-reduce(f32[1024]{0:T(1024)S(1)} %get-tuple-element.1278, f32[512]{0:T(512)S(1)} %reshape.508, f32[1024]{0:T(1024)S(1)} %copy-done.55, f32[1024]{0:T(1024)S(1)} %copy-done.59), channel_id=2, replica_groups=mesh['dp'=8,'grp'=4] {'dp','grp'}, use_global_device_ids=true, to_apply=%region_34.35.clone | all-reduce | flops 3584 | bytes 28672
  607.9 91.2 %reduce-scatter.20.cloned.1.call-done = f32[32,512]{1,0:T(8,128)} async-done(((f32[1024,512]{1,0:T(8,128)}), f32[32,512]{1,0:T(8,128)}) %reduce-scatter.20.cloned.1.call-update) | async-done | bytes 65552 | tf_op jit(solution)/shard_map/reduce_scatter | solution.py:473
  699.1 135.6 %reduce-scatter.18.cloned.1.call-done = f32[32,512]{1,0:T(8,128)} async-done(((f32[1024,512]{1,0:T(8,128)}), f32[32,512]{1,0:T(8,128)}) %reduce-scatter.18.cloned.1.call-update) | async-done | bytes 65552 | tf_op jit(solution)/shard_map/reduce_scatter | solution.py:472
  834.7 139.7 %reduce-scatter.26.cloned.1.call-done = f32[32,1024]{1,0:T(8,128)} async-done(((f32[1024,1024]{1,0:T(8,128)}), f32[32,1024]{1,0:T(8,128)}) %reduce-scatter.26.cloned.1.call-update) | async-done | bytes 131088 | tf_op jit(solution)/shard_map/reduce_scatter | solution.py:480
  974.4 139.9 %reduce-scatter.24.cloned.1.call-done = f32[32,1024]{1,0:T(8,128)} async-done(((f32[1024,1024]{1,0:T(8,128)}), f32[32,1024]{1,0:T(8,128)}) %reduce-scatter.24.cloned.1.call-update) | async-done | bytes 131088 | tf_op jit(solution)/shard_map/reduce_scatter | solution.py:477
  1114.4 139.9 %reduce-scatter.22.cloned.1.call-done = f32[32,1024]{1,0:T(8,128)} async-done(((f32[1024,1024]{1,0:T(8,128)}), f32[32,1024]{1,0:T(8,128)}) %reduce-scatter.22.cloned.1.call-update) | async-done | bytes 131088 | tf_op jit(solution)/shard_map/reduce_scatter | solution.py:474
  1254.3 140.0 %reduce-scatter.16.cloned.1.call-done = f32[32,1024]{1,0:T(8,128)} async-done(((f32[1024,1024]{1,0:T(8,128)}), f32[32,1024]{1,0:T(8,128)}) %reduce-scatter.16.cloned.1.call-update) | async-done | bytes 131088 | tf_op jit(solution)/shard_map/reduce_scatter | solution.py:471
  1394.3 153.6 %reduce-scatter.30.cloned.1.call-done = f32[32,2816]{1,0:T(8,128)} async-done(((f32[1024,2816]{1,0:T(8,128)}), f32[32,2816]{1,0:T(8,128)}) %reduce-scatter.30.cloned.1.call-update) | async-done | bytes 360464 | tf_op jit(solution)/shard_map/reduce_scatter | solution.py:483
  1547.9 155.6 %reduce-scatter.28.cloned.1.call-done = f32[32,2816]{1,0:T(8,128)} async-done(((f32[1024,2816]{1,0:T(8,128)}), f32[32,2816]{1,0:T(8,128)}) %reduce-scatter.28.cloned.1.call-update) | async-done | bytes 360464 | tf_op jit(solution)/shard_map/reduce_scatter | solution.py:482
  1703.5 155.9 %reduce-scatter.32.cloned.1.call-done = f32[88,1024]{1,0:T(8,128)} async-done(((f32[2816,1024]{1,0:T(8,128)}), f32[88,1024]{1,0:T(8,128)}) %reduce-scatter.32.cloned.1.call-update) | async-done | bytes 360464 | tf_op jit(solution)/shard_map/reduce_scatter | solution.py:484
  (465 shorter events, 547.3 us)
Async XLA Ops:
  12.6 18.8 %all-to-all-start.1 = ((bf16[256,4,128]{0,2,1:T(8,128)(2,1)}), bf16[256,4,128]{0,2,1:T(8,128)(2,1)S(1)}, u32[]{:S(2)}, u32[]{:S(2)}) async-start(bf16[256,4,128]{0,2,1:T(8,128)(2,1)} %bitcast.59), calls=%async_computation.1 | async-start | bytes 524288 | tf_op jit(solution)/shard_map/all_to_all | solution.py:354
  31.4 9.5 all-to-all-start.2
  40.9 28.7 %all-to-all-start = ((bf16[256,4,256]{0,2,1:T(8,128)(2,1)}), bf16[256,4,256]{0,2,1:T(8,128)(2,1)S(1)}, u32[]{:S(2)}, u32[]{:S(2)}) async-start(bf16[256,4,256]{0,2,1:T(8,128)(2,1)} %bitcast.57), calls=%async_computation | async-start | bytes 1048576 | tf_op jit(solution)/shard_map/all_to_all | solution.py:353
  136.2 12.3 all-to-all-start.3
  148.5 7.9 all-to-all-start.5
  156.4 7.4 all-to-all-start.6
  163.8 13.1 all-to-all-start.4
  199.7 13.1 all-to-all-start.7
  241.3 13.1 all-to-all-start.8
  245.4 362.5 %reduce-scatter.36.cloned.1.call-start = ((), (), s32[]{:S(2)}) async-start(), calls=%async_computation.37 | async-start | bytes 2162688
  297.0 13.8 all-to-all-start.9
  310.9 9.3 all-to-all-start.14
  320.2 22.2 %all-to-all-start.10 = ((bf16[256,4,256]{0,2,1:T(8,128)(2,1)}), bf16[256,4,256]{0,2,1:T(8,128)(2,1)S(1)}, u32[]{:S(2)}, u32[]{:S(2)}) async-start(bf16[256,4,256]{0,2,1:T(8,128)(2,1)} %bitcast.78), calls=%async_computation.10 | async-start | bytes 1048576 | tf_op jit(solution)/shard_map/all_to_all | solution.py:427
  323.7 284.2 %reduce-scatter.34.cloned.1.call-start = ((), (), s32[]{:S(2)}) async-start(), calls=%async_computation.36 | async-start | bytes 2162688
  342.1 357.0 %reduce-scatter.20.cloned.1.call-start = ((), (), s32[]{:S(2)}) async-start(), calls=%async_computation.29 | async-start | bytes 2162688 | tf_op jit(solution)/shard_map/reduce_scatter | solution.py:473
  478.5 356.2 %reduce-scatter.18.cloned.1.call-start = ((), (), s32[]{:S(2)}) async-start(), calls=%async_computation.28 | async-start | bytes 2162688 | tf_op jit(solution)/shard_map/reduce_scatter | solution.py:472
  492.1 482.4 %reduce-scatter.26.cloned.1.call-start = ((), (), s32[]{:S(2)}) async-start(), calls=%async_computation.32 | async-start | bytes 4325376 | tf_op jit(solution)/shard_map/reduce_scatter | solution.py:480
  496.1 618.2 %reduce-scatter.24.cloned.1.call-start = ((), (), s32[]{:S(2)}) async-start(), calls=%async_computation.31 | async-start | bytes 4325376 | tf_op jit(solution)/shard_map/reduce_scatter | solution.py:477
  501.2 753.0 %reduce-scatter.22.cloned.1.call-start = ((), (), s32[]{:S(2)}) async-start(), calls=%async_computation.30 | async-start | bytes 4325376 | tf_op jit(solution)/shard_map/reduce_scatter | solution.py:474
  505.4 888.9 %reduce-scatter.16.cloned.1.call-start = ((), (), s32[]{:S(2)}) async-start(), calls=%async_computation.27 | async-start | bytes 4325376 | tf_op jit(solution)/shard_map/reduce_scatter | solution.py:471
  522.0 1025.9 %reduce-scatter.30.cloned.1.call-start = ((), (), s32[]{:S(2)}) async-start(), calls=%async_computation.34 | async-start | bytes 11894784 | tf_op jit(solution)/shard_map/reduce_scatter | solution.py:483
  530.4 1173.1 %reduce-scatter.28.cloned.1.call-start = ((), (), s32[]{:S(2)}) async-start(), calls=%async_computation.33 | async-start | bytes 11894784 | tf_op jit(solution)/shard_map/reduce_scatter | solution.py:482
  537.8 1321.5 %reduce-scatter.32.cloned.1.call-start = ((), (), s32[]{:S(2)}) async-start(), calls=%async_computation.35 | async-start | bytes 11894784 | tf_op jit(solution)/shard_map/reduce_scatter | solution.py:484
  557.4 1301.9 %copy-start.1 = (bf16[1024,1024]{1,0:T(8,128)(2,1)S(1)}, bf16[1024,1024]{1,0:T(8,128)(2,1)}, u32[]{:S(2)}) copy-start(bf16[1024,1024]{1,0:T(8,128)(2,1)} %param.50) | copy-start | bytes 6291460
  (70 other events, 967.6 us)
Sparse Core Ops, SparseCore 0:
  289.9 137.9 reduce-scatter.35
  430.8 132.9 reduce-scatter.33
  566.7 132.3 reduce-scatter.19
  701.9 132.7 reduce-scatter.17
  837.4 136.9 reduce-scatter.25
  977.2 137.1 reduce-scatter.23
  1117.2 136.9 reduce-scatter.21
  1257.1 137.1 reduce-scatter.15
  1397.2 150.6 reduce-scatter.29
  1550.6 152.7 reduce-scatter.27
  1706.3 152.9 reduce-scatter.31
where the time goes:
time: 1870 us
  waiting for transfers between devices  1290 us (69%)
  matrix products  188 us (10%)
  local copies, waits for them, and re-layouts  165 us (9%)
  blocking collectives  79.6 us (4%)
  other arithmetic  52.4 us (3%)
  starting transfers between devices  46.8 us (3%)
  loops' own time  28.6 us (2%)
    reduce_scatter x1, waiting for transfers between devices, shards(): lax.psum_scatter(d_ffn_down, ('dp', 'grp'), scatter_dimension=0, tiled=True)  156 us
    reduce_scatter x1, waiting for transfers between devices, shards(): lax.psum_scatter(d_ffn_gate, ('dp', 'grp'), scatter_dimension=0, tiled=True)  156 us
    reduce_scatter x1, waiting for transfers between devices, shards(): lax.psum_scatter(d_ffn_up, ('dp', 'grp'), scatter_dimension=0, tiled=True)  154 us
    reduce_scatter x1, waiting for transfers between devices, shards(): lax.psum_scatter(d_self_query, ('dp', 'grp'), scatter_dimension=0, tiled=...  140 us
    reduce_scatter x1, waiting for transfers between devices, shards(): lax.psum_scatter(d_cross_query, ('dp', 'grp'), scatter_dimension=0, tiled...  140 us
    reduce_scatter x1, waiting for transfers between devices, shards(): lax.psum_scatter(d_self_out, ('dp', 'grp'), scatter_dimension=0, tiled=True)  140 us
    reduce_scatter x1, waiting for transfers between devices, shards(): lax.psum_scatter(d_cross_out, ('dp', 'grp'), scatter_dimension=0, tiled=T...  140 us
    reduce_scatter x1, waiting for transfers between devices, shards(): lax.psum_scatter(d_self_key, ('dp', 'grp'), scatter_dimension=0, tiled=True)  136 us
  transfers between devices with their start and end apart: 23, of which 17 were waited for; matrix products, arithmetic and copies ran while one was open for 14% of the time, Pallas kernels for 0%

commit v1 on v0

v1 whole, which is shorter than its diff:
```python
import functools

import jax
import jax.numpy as jnp
from jax import lax
from jax.experimental import pallas as pl
from jax.experimental.pallas import tpu as pltpu
from jax.sharding import PartitionSpec as P

SHORT = 1024
RATIO = 4
BUCKETS = 32
HEADS = 16
EPSILON = 1e-06
THRESHOLDS = (19, 21, 24, 27, 31, 35, 40, 46, 52, 59, 67, 77, 87, 99, 113)
CORES = 2
BF16 = jnp.bfloat16
F32 = jnp.float32
NEGATIVE = -1e30
HEAD = 64
TILE = 256
NEAR = 128
VMEM_LIMIT = 56 * 1024 * 1024


def dot(a, b):
    return jnp.dot(a, b, preferred_element_type=jnp.float32)


def place_rows(half, at):
    zero = jnp.zeros_like(half)
    return jnp.concatenate([half, zero] if at == 0 else [zero, half], axis=0)


def place_lanes(pair, source, at):
    lane = lax.broadcasted_iota(jnp.int32, pair.shape, 1)
    if source != at:
        pair = jnp.concatenate([pair[:, HEAD:], pair[:, :HEAD]], axis=1)
    return jnp.where((lane < HEAD) == (at == 0), pair, jnp.zeros_like(pair))


def near_tiles(table_row):
    skewed = pltpu.roll(jnp.broadcast_to(table_row, (NEAR, 2 * NEAR)), 0, 1, stride=1, stride_axis=0)
    key_at = lax.broadcasted_iota(jnp.int32, (NEAR, NEAR), 0)
    row_at = lax.broadcasted_iota(jnp.int32, (NEAR, NEAR), 1)
    return (jnp.where(key_at <= row_at, skewed[:, :NEAR], NEGATIVE), skewed[:, NEAR:])


def add_corner(scores, tile):
    rows = scores.shape[0]
    low_rows = scores[rows - NEAR :]
    low_rows = jnp.concatenate([low_rows[:, :NEAR] + tile, low_rows[:, NEAR:]], axis=1)
    return jnp.concatenate([scores[: rows - NEAR], low_rows], axis=0)


def add_diagonal(scores, at_zero, at_one):
    rows = scores.shape[0]
    first = scores[rows - TILE : rows - NEAR]
    second = scores[rows - NEAR :]
    last = [
        jnp.concatenate([first[:, :NEAR] + at_zero, first[:, NEAR:] + at_one], axis=1),
        jnp.concatenate([jnp.full((NEAR, NEAR), NEGATIVE, jnp.float32), second[:, NEAR:] + at_zero], axis=1),
    ]
    if rows > TILE:
        last = [add_corner(scores[: rows - TILE], at_one)] + last
    return jnp.concatenate(last, axis=0)


def by_distance(near):
    level = near[:8]
    for first in range(8, NEAR, 8):
        level = level + pltpu.roll(near[first : first + 8], 2 * NEAR - first, 1)
    row = lax.broadcasted_iota(jnp.int32, level.shape, 0)
    for bit in (1, 2, 4):
        level = jnp.where(row & bit > 0, pltpu.roll(level, 2 * NEAR - bit, 1), level)
    return jnp.sum(level, axis=0, keepdims=True)


def self_forward_kernel(valid_ref, table_ref, q_ref, k_ref, v_ref, kp_ref, vp_ref, o_ref, lse_ref, *, earlier):
    rows = q_ref.shape[0]
    v_turned = v_ref[...].T
    vp_turned = [vp_ref[s].T for s in range(earlier)]
    for e in range(2):
        lanes = pl.ds(e * 2 * HEAD, 2 * HEAD)
        q_turned = q_ref[:, lanes].T
        tiles = [near_tiles(table_ref[0, 2 * e + r : 2 * e + r + 1, :]) for r in range(2)]
        for t in range(rows // TILE):
            cols = slice(t * TILE, (t + 1) * TILE)
            outs = []
            for r in range(2):
                at_zero, at_one = tiles[r]
                q_tile = place_rows(q_turned[r * HEAD : (r + 1) * HEAD, cols], e)
                seen = (t + 1) * TILE
                scores = add_diagonal(dot(k_ref[:seen], q_tile), at_zero, at_one)
                peak = jnp.max(scores, axis=0, keepdims=True)
                weights = jnp.exp(scores - peak)
                summed = jnp.sum(weights, axis=0, keepdims=True)
                acc = dot(v_turned[:, :seen], weights.astype(jnp.bfloat16))[e * HEAD : (e + 1) * HEAD]

                for s in range(earlier):

                    def visit(state, s=s, q_tile=q_tile, at_one=at_one, t=t):
                        peak, summed, acc = state
                        scores = dot(kp_ref[s], q_tile)
                        if s == 0 and t == 0:
                            scores = add_corner(scores, at_one)
                        new_peak = jnp.maximum(peak, jnp.max(scores, axis=0, keepdims=True))
                        rescale = jnp.exp(peak - new_peak)
                        weights = jnp.exp(scores - new_peak)
                        summed = summed * rescale + jnp.sum(weights, axis=0, keepdims=True)
                        add = dot(vp_turned[s], weights.astype(jnp.bfloat16))[e * HEAD : (e + 1) * HEAD]
                        return (new_peak, summed, acc * rescale + add)

                    peak, summed, acc = lax.cond(
                        valid_ref[s] > 0, visit, lambda state: state, (peak, summed, acc)
                    )
                outs.append(acc / summed)
                lse_ref[0, 2 * e + r : 2 * e + r + 1, cols] = peak + jnp.log(summed)
            o_ref[cols, lanes] = jnp.concatenate(outs, axis=0).T.astype(jnp.bfloat16)


def self_forward(valid, table, q, k, v, kp, vp):
    rows = q.shape[0]
    blocks = k.shape[1] // (2 * HEAD)
    earlier = kp.shape[0]
    return pl.pallas_call(
        functools.partial(self_forward_kernel, earlier=earlier),
        grid=(blocks,),
        in_specs=[
            pl.BlockSpec(memory_space=pltpu.SMEM),
            pl.BlockSpec((1, 8, 2 * NEAR), lambda p: (p, 0, 0)),
            pl.BlockSpec((rows, 4 * HEAD), lambda p: (0, p)),
            pl.BlockSpec((rows, 2 * HEAD), lambda p: (0, p)),
            pl.BlockSpec((rows, 2 * HEAD), lambda p: (0, p)),
            pl.BlockSpec((earlier, rows, 2 * HEAD), lambda p: (0, 0, p)),
            pl.BlockSpec((earlier, rows, 2 * HEAD), lambda p: (0, 0, p)),
        ],
        out_specs=[
            pl.BlockSpec((rows, 4 * HEAD), lambda p: (0, p)),
            pl.BlockSpec((1, 8, rows), lambda p: (p, 0, 0)),
        ],
        out_shape=[
            jax.ShapeDtypeStruct(q.shape, jnp.bfloat16),
            jax.ShapeDtypeStruct((blocks, 8, rows), jnp.float32),
        ],
        compiler_params=pltpu.CompilerParams(vmem_limit_bytes=VMEM_LIMIT),
        name="self_forward",
    )(valid, table, q, k, v, kp, vp)


def self_backward_kernel(
    valid_ref, table_ref, q_ref, k_ref, v_ref, kp_ref, vp_ref, do_ref, o_ref, lse_ref,
    dq_ref, dk_ref, dv_ref, dkp_ref, dvp_ref, db_ref, total_ref,
    dk_sum, dv_sum, dkp_sum, dvp_sum, near_sum, *, earlier,
):
    rows = q_ref.shape[0]
    dk_sum[...] = jnp.zeros_like(dk_sum)
    dv_sum[...] = jnp.zeros_like(dv_sum)
    dkp_sum[...] = jnp.zeros_like(dkp_sum)
    dvp_sum[...] = jnp.zeros_like(dvp_sum)
    k_turned = k_ref[...].T
    kp_turned = [kp_ref[s].T for s in range(earlier)]
    for e in range(2):
        lanes = pl.ds(e * 2 * HEAD, 2 * HEAD)
        q_pair = q_ref[:, lanes]
        do_pair = do_ref[:, lanes]
        q_turned = q_pair.T
        do_turned = do_pair.T
        product = (do_pair.astype(jnp.float32) * o_ref[:, lanes].astype(jnp.float32)).T
        half = slice(e * HEAD, (e + 1) * HEAD)
        tiles = [near_tiles(table_ref[0, 2 * e + r : 2 * e + r + 1, :]) for r in range(2)]
        q_placed = [place_lanes(q_pair, r, e) for r in range(2)]
        do_placed = [place_lanes(do_pair, r, e) for r in range(2)]
        totals = [jnp.zeros((1, TILE), jnp.float32) for _ in range(2)]
        for t in range(rows // TILE):
            cols = slice(t * TILE, (t + 1) * TILE)
            d_queries = []
            for r in range(2):
                at_zero, at_one = tiles[r]
                head = slice(r * HEAD, (r + 1) * HEAD)
                q_tile_t = place_rows(q_turned[head, cols], e)
                do_tile_t = place_rows(do_turned[head, cols], e)
                q_tile = q_placed[r][cols]
                do_tile = do_placed[r][cols]
                delta = jnp.sum(product[head, cols], axis=0, keepdims=True)
                lse = lse_ref[0, 2 * e + r : 2 * e + r + 1, cols]

                def one(scores, v_rows, lse=lse, delta=delta, do_tile_t=do_tile_t):
                    prob = jnp.exp(scores - lse)
                    d_prob = dot(v_rows, do_tile_t)
                    d_score = prob * (d_prob - delta)
                    return prob.astype(jnp.bfloat16), d_score.astype(jnp.bfloat16)

                seen = (t + 1) * TILE
                scores = add_diagonal(dot(k_ref[:seen], q_tile_t), at_zero, at_one)
                prob, d_score = one(scores, v_ref[:seen])
                dv_sum[:seen] += dot(prob, do_tile)
                dk_sum[:seen] += dot(d_score, q_tile)
                d_query = dot(k_turned[:, :seen], d_score)[half]
                d_wide = d_score.astype(jnp.float32)
                totals[r] = totals[r] + jnp.sum(d_wide, axis=0, keepdims=True)
                base = seen - TILE
                zero_part = d_wide[base : base + NEAR, :NEAR] + d_wide[base + NEAR :, NEAR:]
                one_part = d_wide[base : base + NEAR, NEAR:]
                if t > 0:
                    one_part = one_part + d_wide[base - NEAR : base, :NEAR]
                both = jnp.concatenate([zero_part, one_part], axis=1)
                if t == 0:
                    near_sum[r] = both
                else:
                    near_sum[r] += both
                for s in range(earlier):

                    def visit(state, s=s, t=t, r=r, q_tile_t=q_tile_t, q_tile=q_tile, do_tile=do_tile, at_one=at_one, one=one):
                        d_query, total = state
                        scores = dot(kp_ref[s], q_tile_t)
                        if s == 0 and t == 0:
                            scores = add_corner(scores, at_one)
                        prob, d_score = one(scores, vp_ref[s])
                        dvp_sum[s] += dot(prob, do_tile)
                        dkp_sum[s] += dot(d_score, q_tile)
                        d_query = d_query + dot(kp_turned[s], d_score)[half]
                        d_wide = d_score.astype(jnp.float32)
                        if s == 0 and t == 0:
                            near_sum[r, :, NEAR:] += d_wide[rows - NEAR :, :NEAR]
                        return (d_query, total + jnp.sum(d_wide, axis=0, keepdims=True))

                    d_query, totals[r] = lax.cond(
                        valid_ref[s] > 0, visit, lambda state: state, (d_query, totals[r])
                    )
                d_queries.append(d_query)
            dq_ref[cols, lanes] = jnp.concatenate(d_queries, axis=0).T.astype(jnp.bfloat16)
        for r in range(2):
            db_ref[0, 2 * e + r : 2 * e + r + 1, :] = by_distance(near_sum[r])
            total_ref[0, 2 * e + r : 2 * e + r + 1, :] = totals[r]
    dk_ref[...] = dk_sum[...].astype(jnp.bfloat16)
    dv_ref[...] = dv_sum[...].astype(jnp.bfloat16)
    dkp_ref[...] = dkp_sum[...].astype(jnp.bfloat16)
    dvp_ref[...] = dvp_sum[...].astype(jnp.bfloat16)


def self_backward(valid, table, q, k, v, kp, vp, do, o, lse):
    rows = q.shape[0]
    blocks = k.shape[1] // (2 * HEAD)
    earlier = kp.shape[0]
    wide = pl.BlockSpec((rows, 4 * HEAD), lambda p: (0, p))
    slim = pl.BlockSpec((rows, 2 * HEAD), lambda p: (0, p))
    past = pl.BlockSpec((earlier, rows, 2 * HEAD), lambda p: (0, 0, p))
    tab = pl.BlockSpec((1, 8, 2 * NEAR), lambda p: (p, 0, 0))
    return pl.pallas_call(
        functools.partial(self_backward_kernel, earlier=earlier),
        grid=(blocks,),
        in_specs=[
            pl.BlockSpec(memory_space=pltpu.SMEM), tab, wide, slim, slim, past, past, wide, wide,
            pl.BlockSpec((1, 8, rows), lambda p: (p, 0, 0)),
        ],
        out_specs=[wide, slim, slim, past, past, tab, tab],
        out_shape=[
            jax.ShapeDtypeStruct(q.shape, jnp.bfloat16),
            jax.ShapeDtypeStruct(k.shape, jnp.bfloat16),
            jax.ShapeDtypeStruct(k.shape, jnp.bfloat16),
            jax.ShapeDtypeStruct(kp.shape, jnp.bfloat16),
            jax.ShapeDtypeStruct(kp.shape, jnp.bfloat16),
            jax.ShapeDtypeStruct(table.shape, jnp.float32),
            jax.ShapeDtypeStruct(table.shape, jnp.float32),
        ],
        scratch_shapes=[
            pltpu.VMEM((rows, 2 * HEAD), jnp.float32),
            pltpu.VMEM((rows, 2 * HEAD), jnp.float32),
            pltpu.VMEM((earlier, rows, 2 * HEAD), jnp.float32),
            pltpu.VMEM((earlier, rows, 2 * HEAD), jnp.float32),
            pltpu.VMEM((2, NEAR, 2 * NEAR), jnp.float32),
        ],
        compiler_params=pltpu.CompilerParams(vmem_limit_bytes=VMEM_LIMIT),
        name="self_backward",
    )(valid, table, q, k, v, kp, vp, do, o, lse)


def cross_forward_kernel(q_ref, k_ref, v_ref, own_ref, o_ref, lse_ref, *, masked):
    rows = q_ref.shape[0]
    v_turned = v_ref[...].T
    if masked:
        blocked = jnp.where(own_ref[...] > 0, 0.0, NEGATIVE)
    for e in range(2):
        lanes = pl.ds(e * 2 * HEAD, 2 * HEAD)
        q_turned = q_ref[:, lanes].T
        for t in range(rows // TILE):
            cols = slice(t * TILE, (t + 1) * TILE)
            outs = []
            for r in range(2):
                q_tile = place_rows(q_turned[r * HEAD : (r + 1) * HEAD, cols], e)
                scores = dot(k_ref[...], q_tile)
                if masked:
                    scores = scores + blocked
                peak = jnp.max(scores, axis=0, keepdims=True)
                weights = jnp.exp(scores - peak)
                summed = jnp.sum(weights, axis=0, keepdims=True)
                acc = dot(v_turned, weights.astype(jnp.bfloat16))[e * HEAD : (e + 1) * HEAD]
                outs.append(acc / summed)
                lse_ref[0, 2 * e + r : 2 * e + r + 1, cols] = peak + jnp.log(summed)
            o_ref[cols, lanes] = jnp.concatenate(outs, axis=0).T.astype(jnp.bfloat16)


def cross_forward(q, k, v, own, masked):
    rows, keys = q.shape[0], k.shape[0]
    blocks = k.shape[1] // (2 * HEAD)
    wide = pl.BlockSpec((rows, 4 * HEAD), lambda p: (0, p))
    slim = pl.BlockSpec((keys, 2 * HEAD), lambda p: (0, p))
    return pl.pallas_call(
        functools.partial(cross_forward_kernel, masked=masked),
        grid=(blocks,),
        in_specs=[wide, slim, slim, pl.BlockSpec(own.shape, lambda p: (0, 0))],
        out_specs=[wide, pl.BlockSpec((1, 8, rows), lambda p: (p, 0, 0))],
        out_shape=[
            jax.ShapeDtypeStruct(q.shape, jnp.bfloat16),
            jax.ShapeDtypeStruct((blocks, 8, rows), jnp.float32),
        ],
        compiler_params=pltpu.CompilerParams(vmem_limit_bytes=VMEM_LIMIT),
        name="cross_forward",
    )(q, k, v, own)


def cross_backward_kernel(q_ref, k_ref, v_ref, own_ref, do_ref, o_ref, lse_ref, dq_ref, dk_ref, dv_ref, dk_sum, dv_sum, *, masked):
    rows = q_ref.shape[0]
    dk_sum[...] = jnp.zeros_like(dk_sum)
    dv_sum[...] = jnp.zeros_like(dv_sum)
    k_turned = k_ref[...].T
    if masked:
        blocked = jnp.where(own_ref[...] > 0, 0.0, NEGATIVE)
    for e in range(2):
        lanes = pl.ds(e * 2 * HEAD, 2 * HEAD)
        q_pair = q_ref[:, lanes]
        do_pair = do_ref[:, lanes]
        q_turned = q_pair.T
        do_turned = do_pair.T
        product = (do_pair.astype(jnp.float32) * o_ref[:, lanes].astype(jnp.float32)).T
        half = slice(e * HEAD, (e + 1) * HEAD)
        for t in range(rows // TILE):
            cols = slice(t * TILE, (t + 1) * TILE)
            d_queries = []
            for r in range(2):
                head = slice(r * HEAD, (r + 1) * HEAD)
                scores = dot(k_ref[...], place_rows(q_turned[head, cols], e))
                if masked:
                    scores = scores + blocked
                delta = jnp.sum(product[head, cols], axis=0, keepdims=True)
                prob = jnp.exp(scores - lse_ref[0, 2 * e + r : 2 * e + r + 1, cols])
                d_prob = dot(v_ref[...], place_rows(do_turned[head, cols], e))
                d_score = (prob * (d_prob - delta)).astype(jnp.bfloat16)
                dv_sum[...] += dot(prob.astype(jnp.bfloat16), place_lanes(do_pair[cols], r, e))
                dk_sum[...] += dot(d_score, place_lanes(q_pair[cols], r, e))
                d_queries.append(dot(k_turned, d_score)[half])
            dq_ref[cols, lanes] = jnp.concatenate(d_queries, axis=0).T.astype(jnp.bfloat16)
    dk_ref[...] = dk_sum[...].astype(jnp.bfloat16)
    dv_ref[...] = dv_sum[...].astype(jnp.bfloat16)


def cross_backward(q, k, v, own, do, o, lse, masked):
    rows, keys = q.shape[0], k.shape[0]
    blocks = k.shape[1] // (2 * HEAD)
    wide = pl.BlockSpec((rows, 4 * HEAD), lambda p: (0, p))
    slim = pl.BlockSpec((keys, 2 * HEAD), lambda p: (0, p))
    return pl.pallas_call(
        functools.partial(cross_backward_kernel, masked=masked),
        grid=(blocks,),
        in_specs=[wide, slim, slim, pl.BlockSpec(own.shape, lambda p: (0, 0)), wide, wide, pl.BlockSpec((1, 8, rows), lambda p: (p, 0, 0))],
        out_specs=[wide, slim, slim],
        out_shape=[
            jax.ShapeDtypeStruct(q.shape, jnp.bfloat16),
            jax.ShapeDtypeStruct(k.shape, jnp.bfloat16),
            jax.ShapeDtypeStruct(k.shape, jnp.bfloat16),
        ],
        scratch_shapes=[pltpu.VMEM((keys, 2 * HEAD), jnp.float32), pltpu.VMEM((keys, 2 * HEAD), jnp.float32)],
        compiler_params=pltpu.CompilerParams(vmem_limit_bytes=VMEM_LIMIT),
        name="cross_backward",
    )(q, k, v, own, do, o, lse)


def place_of(position, order):
    spot = jnp.int32(0)
    for bit in order:
        spot = spot * 2 + jnp.bitwise_and(lax.shift_right_logical(position, jnp.int32(bit)), 1)
    return spot


def weight_kernel(place_ref, *refs, n_x, n_y, columns, chunk, order):
    x_refs, y_refs = refs[:n_x], refs[n_x : n_x + n_y]
    send_ref, keep_ref = refs[n_x + n_y :]
    half = 1 << (len(order) - 1)
    chip, core = place_ref[0], place_ref[1]
    turned = [x_ref[...].T for x_ref in x_refs]
    start = 0
    for terms in columns:
        width = y_refs[terms[0][1]].shape[1]
        cols = slice(start, start + width)
        start += width
        parts = len(terms[0][0])
        for part in range(parts):
            part_rows = turned[terms[0][0][part]].shape[0]
            step = part_rows
            while step > 512 and step % (2 * chunk) == 0:
                step //= 2
            per_part = part_rows // chunk
            for first in range(0, part_rows, step):
                tile = None
                for x_ids, y_id in terms:
                    term = dot(turned[x_ids[part]][first : first + step], y_refs[y_id][...])
                    tile = term if tile is None else tile + term
                tile = tile.astype(BF16)
                for inner in range(step // chunk):
                    number = jnp.int32(first // chunk + inner)
                    if parts == 2:
                        number = number + (core if part == 0 else 1 - core) * per_part
                    spot = place_of(jnp.bitwise_xor(number, chip), order)
                    piece = tile[inner * chunk : (inner + 1) * chunk]

                    @pl.when(spot >= half)
                    def _(spot=spot, piece=piece, cols=cols):
                        send_ref[spot - half, :, cols] = piece

                    @pl.when(spot < half)
                    def _(spot=spot, piece=piece, cols=cols):
                        keep_ref[spot, :, cols] = piece


def weight_sums(place, xs, ys, columns, rows_out, order, name):
    chips = 1 << len(order)
    chunk = rows_out // chips
    width = sum(ys[terms[0][1]].shape[1] for terms in columns)
    half = chips // 2
    if chunk % 16:
        pieces = []
        for terms in columns:
            total = 0.0
            for x_ids, y_id in terms:
                parts = [matmul_left(xs[x], ys[y_id]) for x in x_ids]
                if len(parts) == 2:
                    parts = [jnp.where(place[1] == 0, parts[0], parts[1]), jnp.where(place[1] == 0, parts[1], parts[0])]
                total = total + jnp.concatenate(parts, axis=0)
            pieces.append(total.astype(BF16))
        whole = jnp.concatenate(pieces, axis=1).reshape(chips, chunk, width)
        where = jnp.arange(chips, dtype=jnp.int32)
        position = sum((((where >> (len(order) - 1 - at)) & 1) << bit) for at, bit in enumerate(order))
        whole = jnp.take(whole, jnp.bitwise_xor(position, place[0]), axis=0)
        return whole[half:], whole[:half]
    full = lambda a: pl.BlockSpec(a.shape, lambda i, p: (0, 0))
    flops = 2 * sum(xs[0].shape[0] * rows_out * ys[y].shape[1] for terms in columns for _, y in terms)
    out = jax.ShapeDtypeStruct((half, chunk, width), BF16)
    spec = pl.BlockSpec((half, chunk, width), lambda i, p: (0, 0, 0))
    return pl.pallas_call(
        functools.partial(weight_kernel, n_x=len(xs), n_y=len(ys), columns=columns, chunk=chunk, order=order),
        grid_spec=pltpu.PrefetchScalarGridSpec(
            num_scalar_prefetch=1,
            grid=(1,),
            in_specs=[full(a) for a in xs + ys],
            out_specs=[spec, spec],
        ),
        out_shape=[out, out],
        compiler_params=pltpu.CompilerParams(vmem_limit_bytes=VMEM_LIMIT),
        cost_estimate=pl.CostEstimate(
            flops=flops, bytes_accessed=2 * (sum(a.size for a in xs + ys) + rows_out * width), transcendentals=0
        ),
        name=name,
    )(place, *xs, *ys)


def matmul_left(a, b):
    return lax.dot_general(a, b, (((0,), (0,)), ((), ())), preferred_element_type=F32)


def matmul_right(a, b):
    return lax.dot_general(a, b, (((1,), (1,)), ((), ())), preferred_element_type=F32)


def rel_bucket(distance):
    beyond = 16 + sum((distance >= border).astype(jnp.int32) for border in THRESHOLDS)
    return jnp.where(distance < 16, distance, beyond)


def inverse_norm(hidden):
    return lax.rsqrt(jnp.mean(hidden * hidden, axis=-1, keepdims=True) + EPSILON)


def norm_low(hidden, inverse, gain):
    return (hidden * inverse * gain).astype(BF16)


def norm_back(hidden, inverse, gain, dz):
    scaled = gain * dz
    inner = jnp.mean(scaled * hidden, axis=-1, keepdims=True)
    return inverse * scaled - hidden * (inverse * inverse * inverse) * inner


def gain_sum(hidden, inverse, dz):
    return jnp.sum(dz * hidden * inverse, axis=0)


def shards(
    tokens, memory, cotangent, bucket, gain_self, self_query, self_key, self_value, self_out, rel_bias,
    gain_cross, cross_query, cross_key, cross_value, cross_out, gain_ffn, ffn_gate, ffn_up, ffn_down,
):
    groups = lax.axis_size("grp")
    dp_size = lax.axis_size("dp")
    n_chips = groups // CORES
    chips = dp_size * n_chips
    grp_at = lax.axis_index("grp")
    core = grp_at % CORES
    y_at = grp_at // CORES
    chip = lax.axis_index("dp") * n_chips + y_at
    place = jnp.stack([chip, core]).astype(jnp.int32)
    rows = tokens.shape[0]
    chip_rows = rows * CORES
    group_rows = chip_rows * n_chips
    mem_rows = memory.shape[0]
    length = jnp.minimum(group_rows, jnp.maximum(SHORT, jnp.right_shift(jnp.int32(group_rows), bucket[0])))
    masked = group_rows > SHORT
    y_bits = n_chips.bit_length() - 1
    bits = chips.bit_length() - 1

    def swap_core(v):
        return lax.ppermute(v, "grp", [(g, g ^ 1) for g in range(groups)])

    def swap_chip(v, bit):
        return lax.ppermute(v, ("dp", "grp"), [(i, i ^ (CORES << bit)) for i in range(chips * CORES)])

    def in_order(own, peer, axis=0):
        return jnp.where(core == 0, jnp.concatenate([own, peer], axis), jnp.concatenate([peer, own], axis))

    def part_of(v, at, axis):
        size = v.shape[axis] // CORES
        return lax.dynamic_slice_in_dim(v, at * size, size, axis)

    gain_one, gain_two, gain_three = (g.astype(F32) for g in (gain_self, gain_cross, gain_ffn))

    tokens_peer = swap_core(tokens)
    past_own = [
        lax.ppermute(tokens, "grp", [(g, g + CORES * s) for g in range(groups - CORES * s)]) for s in range(1, n_chips)
    ]
    cot_peer = swap_core(cotangent)
    mem_all = in_order(memory, swap_core(memory))
    for bit in range(y_bits):
        other = lax.ppermute(mem_all, "grp", [(g, g ^ (CORES << bit)) for g in range(groups)])
        low_first = jnp.concatenate([mem_all, other], 0)
        mem_all = jnp.where((y_at >> bit) & 1 == 0, low_first, jnp.concatenate([other, mem_all], 0))
    past_tokens = [in_order(own, swap_core(own)) for own in past_own]

    distances = jnp.arange(2 * NEAR, dtype=jnp.int32)
    onehot = (rel_bucket(distances)[:, None] == jnp.arange(BUCKETS, dtype=jnp.int32)).astype(F32)
    rel_local = part_of(rel_bias.astype(F32), core, 1)
    heads = rel_local.shape[1]
    by_dist = jnp.dot(onehot, rel_local - rel_local[BUCKETS - 1 :], precision=lax.Precision.HIGHEST)
    table = jnp.pad(by_dist.T.reshape(heads // 4, 4, 2 * NEAR), ((0, 0), (0, 4), (0, 0)))

    hidden_in = in_order(tokens, tokens_peer).astype(F32)
    inv_one = inverse_norm(hidden_in)
    low_one = norm_low(hidden_in, inv_one, gain_one)
    w_key, w_value = part_of(self_key, core, 1), part_of(self_value, core, 1)
    q = dot(low_one, part_of(self_query, core, 1)).astype(BF16)
    k = dot(low_one, w_key).astype(BF16)
    v = dot(low_one, w_value).astype(BF16)
    low_past = []
    for past in past_tokens:
        wide = past.astype(F32)
        low_past.append(norm_low(wide, inverse_norm(wide), gain_one))
    k_past = jnp.stack([dot(low, w_key).astype(BF16) for low in low_past])
    v_past = jnp.stack([dot(low, w_value).astype(BF16) for low in low_past])
    first_chip = y_at * chip_rows // length * length // chip_rows
    valid = jnp.stack([(y_at - s >= first_chip).astype(jnp.int32) for s in range(1, n_chips)])
    att, lse_self = self_forward(valid, table, q, k, v, k_past, v_past)
    att_peer = swap_core(att)
    hidden_mid = hidden_in + dot(att, part_of(self_out, core, 0)) + dot(att_peer, part_of(self_out, 1 - core, 0))

    inv_two = inverse_norm(hidden_mid)
    low_two = norm_low(hidden_mid, inv_two, gain_two)
    cq = dot(low_two, part_of(cross_query, core, 1)).astype(BF16)
    w_ckey, w_cvalue = part_of(cross_key, core, 1), part_of(cross_value, core, 1)
    km = dot(mem_all, w_ckey).astype(BF16)
    vm = dot(mem_all, w_cvalue).astype(BF16)
    mem_doc = jnp.arange(mem_all.shape[0], dtype=jnp.int32) // (length // RATIO)
    own_doc = jnp.broadcast_to((mem_doc == y_at * chip_rows // length).astype(F32)[:, None], (mem_all.shape[0], TILE))
    crs, lse_cross = cross_forward(cq, km, vm, own_doc, masked)
    crs_peer = swap_core(crs)
    hidden_late = hidden_mid + dot(crs, part_of(cross_out, core, 0)) + dot(crs_peer, part_of(cross_out, 1 - core, 0))

    inv_three = inverse_norm(hidden_late)
    low_three = norm_low(hidden_late, inv_three, gain_three)
    w_gate, w_up = part_of(ffn_gate, core, 1), part_of(ffn_up, core, 1)
    gate = dot(low_three, w_gate)
    up = dot(low_three, w_up)
    cot = in_order(cotangent, cot_peer)
    d_inner = matmul_right(cot, part_of(ffn_down, core, 0)).astype(BF16).astype(F32)
    inner, gated_back = jax.vjp(lambda g, u: jax.nn.gelu(g, approximate=True) * u, gate, up)
    inner = inner.astype(BF16)
    d_gate, d_up = (d.astype(BF16) for d in gated_back(d_inner))
    inner_peer = swap_core(inner)
    dz_part = (matmul_right(d_gate, w_gate) + matmul_right(d_up, w_up)).astype(BF16)
    dz_peer = swap_core(dz_part)
    layer_out = (
        part_of(hidden_late, core, 0)
        + dot(part_of(inner, core, 0), part_of(ffn_down, core, 0))
        + dot(part_of(inner_peer, core, 0), part_of(ffn_down, 1 - core, 0))
    ).astype(BF16)

    x_bit, z_bit, far_bits = y_bits, y_bits + 1, tuple(range(y_bits + 2, bits))
    y_order = tuple(range(y_bits))
    orders = (
        (x_bit,) + y_order + (z_bit,) + far_bits,
        y_order + (z_bit, x_bit) + far_bits,
        (z_bit, x_bit) + y_order + far_bits,
    )

    def column_half(v):
        return part_of(v, core, 1)

    sums = {}
    model = low_one.shape[1]
    hidden_units = ffn_down.shape[0]
    sums["down"] = (
        weight_sums(place, [inner, inner_peer], [column_half(cot)], [[((0, 1), 0)]], hidden_units, orders[2], "down_sums"),
        orders[2],
    )
    sums["gate"] = (weight_sums(place, [low_three], [d_gate], [[((0,), 0)]], model, orders[0], "gate_sums"), orders[0])
    sums["up"] = (weight_sums(place, [low_three], [d_up], [[((0,), 0)]], model, orders[1], "up_sums"), orders[1])
    dz = dz_part.astype(F32) + dz_peer.astype(F32)
    d_gain_three = gain_sum(hidden_late, inv_three, dz)
    g_late = cot.astype(F32) + norm_back(hidden_late, inv_three, gain_three, dz)
    late_low = g_late.astype(BF16)

    d_crs = matmul_right(late_low, part_of(cross_out, core, 0)).astype(BF16)
    dcq, dkm, dvm = cross_backward(cq, km, vm, own_doc, d_crs, crs, lse_cross, masked)
    dcq_peer = swap_core(dcq)
    dz = matmul_right(dcq, part_of(cross_query, core, 1)) + matmul_right(dcq_peer, part_of(cross_query, 1 - core, 1))
    d_gain_two = gain_sum(hidden_mid, inv_two, dz)
    g_mid = g_late + norm_back(hidden_mid, inv_two, gain_two, dz)
    mid_low = g_mid.astype(BF16)
    sums["cross"] = (
        weight_sums(
            place,
            [crs, crs_peer, low_two, mem_all, att, att_peer],
            [column_half(late_low), dcq, dkm, dvm, column_half(mid_low)],
            [[((0, 1), 0)], [((2,), 1)], [((3,), 2)], [((3,), 3)], [((4, 5), 4)]],
            model,
            orders[0],
            "cross_sums",
        ),
        orders[0],
    )
    grad_mem = (matmul_right(dkm, w_ckey) + matmul_right(dvm, w_cvalue)).astype(BF16)
    grad_mem = grad_mem.reshape(groups, mem_rows, model)
    grad_mem = jnp.take(grad_mem, jnp.bitwise_xor(jnp.arange(groups, dtype=jnp.int32), grp_at), axis=0)
    for bit in reversed(range(y_bits + 1)):
        half = grad_mem.shape[0] // 2
        got = lax.ppermute(grad_mem[half:], "grp", [(g, g ^ (1 << bit)) for g in range(groups)])
        grad_mem = (grad_mem[:half].astype(F32) + got.astype(F32)).astype(BF16)
    grad_memory = grad_mem[0]

    d_att = matmul_right(mid_low, part_of(self_out, core, 0)).astype(BF16)
    dq, dk, dv, dk_past, dv_past, d_near, d_total = self_backward(
        valid, table, q, k, v, k_past, v_past, d_att, att, lse_self
    )
    self_terms_x = [low_one] + low_past
    sums["self"] = (
        weight_sums(
            place,
            self_terms_x,
            [dq, dk, dv] + [dk_past[s] for s in range(n_chips - 1)] + [dv_past[s] for s in range(n_chips - 1)],
            [
                [((0,), 0)],
                [((0,), 1)] + [((1 + s,), 3 + s) for s in range(n_chips - 1)],
                [((0,), 2)] + [((1 + s,), 2 + n_chips + s) for s in range(n_chips - 1)],
            ],
            model,
            orders[1],
            "self_sums",
        ),
        orders[1],
    )
    dkv_total = jnp.concatenate([dk, dv], axis=1).astype(F32)
    for s in range(1, n_chips):
        both = jnp.concatenate([dk_past[s - 1], dv_past[s - 1]], axis=1)
        dkv_total = dkv_total + lax.ppermute(
            both, "grp", [(g, g - CORES * s) for g in range(CORES * s, groups)]
        ).astype(F32)
    dkv_total = dkv_total.astype(BF16)
    kv_cols = dk.shape[1]
    dz_part = (
        matmul_right(dq, part_of(self_query, core, 1))
        + matmul_right(dkv_total[:, :kv_cols], w_key)
        + matmul_right(dkv_total[:, kv_cols:], w_value)
    )
    dz_got = swap_core(part_of(dz_part, 1 - core, 0).astype(BF16))
    dz = part_of(dz_part, core, 0) + dz_got.astype(F32)
    own_in = tokens.astype(F32)
    own_inv = inverse_norm(own_in)
    d_gain_one = gain_sum(own_in, own_inv, dz)
    grad_tokens = (part_of(g_mid, core, 0) + norm_back(own_in, own_inv, gain_one, dz)).astype(BF16)

    near = d_near[:, :4].reshape(heads, 2 * NEAR)
    total = jnp.sum(d_total[:, :4], axis=-1).reshape(heads)
    by_bucket = jnp.dot(near, onehot, precision=lax.Precision.HIGHEST)
    far = total - jnp.sum(near, axis=1)
    by_bucket = by_bucket + far[:, None] * onehot[2 * NEAR - 1]
    rel_grad = lax.dynamic_update_slice(jnp.zeros((BUCKETS, HEADS), F32), by_bucket.T, (jnp.int32(0), core * heads))
    small = jnp.concatenate(
        [
            d_gain_one.reshape(chips, -1),
            jnp.where(core == 0, d_gain_two, 0.0).reshape(chips, -1),
            jnp.where(core == 0, d_gain_three, 0.0).reshape(chips, -1),
            rel_grad.reshape(chips, -1),
        ],
        axis=1,
    )
    small = jnp.take(small, jnp.bitwise_xor(jnp.arange(chips, dtype=jnp.int32), chip), axis=0)
    for bit in reversed(range(bits)):
        half = small.shape[0] // 2
        small = small[:half] + swap_chip(small[half:], bit)
    small = small[0]
    gain_cols = model // chips

    def core_share(vec, at):
        return part_of(vec, at, 0)

    pieces = [small[i * gain_cols : (i + 1) * gain_cols] for i in range(3)] + [small[3 * gain_cols :]]
    mine = jnp.concatenate([core_share(piece, core) for piece in pieces])
    other = jnp.concatenate([core_share(piece, 1 - core) for piece in pieces])
    mine = mine + swap_core(other)
    gain_share = gain_cols // CORES
    small_out = [mine[i * gain_share : (i + 1) * gain_share] for i in range(3)] + [mine[3 * gain_share :]]

    done = {}
    for name, ((send, keep), order) in sums.items():
        for at, bit in enumerate(order):
            got = swap_chip(send, bit)
            if at + 1 < len(order):
                half = keep.shape[0] // 2
                send = (keep[half:].astype(F32) + got[half:].astype(F32)).astype(BF16)
                keep = (keep[:half].astype(F32) + got[:half].astype(F32)).astype(BF16)
            else:
                keep = keep.astype(F32) + got.astype(F32)
        result = keep[0]
        peer = swap_core(part_of(result, 1 - core, 0).astype(BF16)).astype(F32)
        done[name] = (part_of(result, core, 0), peer)

    def columns_of(name, start, width):
        own, peer = (v[:, start : start + width] for v in done[name])
        return in_order(own, peer, 1)

    wide = model // 2
    slim = self_key.shape[1] // 2
    ff = hidden_units // 2
    return (
        layer_out,
        grad_tokens,
        grad_memory,
        small_out[0],
        columns_of("self", 0, wide),
        columns_of("self", wide, slim),
        columns_of("self", wide + slim, slim),
        columns_of("cross", 2 * wide + 2 * slim, wide),
        small_out[3],
        small_out[1],
        columns_of("cross", wide, wide),
        columns_of("cross", 2 * wide, slim),
        columns_of("cross", 2 * wide + slim, slim),
        columns_of("cross", 0, wide),
        small_out[2],
        columns_of("gate", 0, ff),
        columns_of("up", 0, ff),
        columns_of("down", 0, wide),
    )


def solution(mesh):
    rows = P(("dp", "grp"), None)
    flat = P(("dp", "grp"))
    in_specs = (rows, rows, rows, P("dp")) + (P(),) * 15
    out_specs = (rows,) * 3 + (flat,) + (rows,) * 4 + (flat,) * 2 + (rows,) * 4 + (flat,) + (rows,) * 3
    return jax.shard_map(shards, mesh=mesh, in_specs=in_specs, out_specs=out_specs, check_vma=False)
```

time: 1870 us -> 345 us (0.18)
  waiting for transfers between devices: 1290 us -> 92.9 us
  local copies, waits for them, and re-layouts: 165 us -> 11.5 us
  matrix products: 188 us -> 48.3 us
  blocking collectives: 79.6 us -> 0 us
  Pallas kernels: 0 us -> 75.8 us
  loops' own time: 28.6 us -> 0 us
    reduce_scatter x9 -> x0, waiting for transfers between devices: 1250 us -> none  [the longest x1 156 us: shards(): lax.psum_scatter(d_ffn_down, ('dp', 'grp'), scatter_dimension=0, tiled=True)]
    dot_general x72 -> x30, matrix products: 188 us -> 48.3 us  [the longest x16 28.3 us: dot(): return jnp.dot(a, b, preferred_element_type=jnp.float32)]
    ppermute x0 -> x45, waiting for transfers between devices: none -> 92.9 us  [the longest x24 65.4 us: swap_chip(): lax.ppermute(v, ('dp', 'grp'), [(i, i ^ CORES << bit) for i in range(chip...]
    pallas_call x0 -> x9, Pallas kernels: none -> 75.8 us  [the longest x5 40.7 us: weight_sums(): pl.pallas_call(functools.partial(weight_kernel, n_x=len(xs), n_y=len(ys),...]
    ppermute x0 -> x45, starting transfers between devices: none -> 51.1 us  [the longest x24 41.3 us: swap_chip(): lax.ppermute(v, ('dp', 'grp'), [(i, i ^ CORES << bit) for i in range(chip...]
    all_to_all x12 -> x0, starting transfers between devices: 45.3 us -> none  [the longest x1 4.24 us: shards(): lax.all_to_all(key_rows, 'grp', split_axis=1, concat_axis=0, tiled=True)]
    unnamed x1 -> x0, blocking collectives: 42 us -> none
    all_to_all x12 -> x0, waiting for transfers between devices: 38.9 us -> none  [the longest x1 8.88 us: shards(): lax.all_to_all(crossed, 'grp', split_axis=0, concat_axis=1, tiled=True)]
  transfers between devices with their start and end apart: 23 -> 45, of which waited for: 17 -> 20; matrix products, arithmetic and copies ran while one was open for 14% -> 30% of each run, Pallas kernels for 0% -> 22%
where the time goes in v1:
time: 345 us; the launch traced here: 341 us
  waiting for transfers between devices  92.9 us (27%)
  Pallas kernels  75.8 us (22%)
  other arithmetic  58.9 us (17%)
  starting transfers between devices  51.1 us (15%)
  matrix products  48.3 us (14%)
  local copies, waits for them, and re-layouts  11.5 us (3%)
    ppermute x24, waiting for transfers between devices, swap_chip(): lax.ppermute(v, ('dp', 'grp'), [(i, i ^ CORES << bit) for i in range(chip...  65.4 us
    ppermute x24, starting transfers between devices, swap_chip(): lax.ppermute(v, ('dp', 'grp'), [(i, i ^ CORES << bit) for i in range(chip...  41.3 us
    pallas_call x5, Pallas kernels, weight_sums(): pl.pallas_call(functools.partial(weight_kernel, n_x=len(xs), n_y=len(ys),...  40.7 us
    dot_general x16, matrix products, dot(): return jnp.dot(a, b, preferred_element_type=jnp.float32)  28.3 us
    dot_general x12, matrix products, matmul_right(): lax.dot_general(a, b, (((1,), (1,)), ((), ())), preferred_element_type=F32)  18.9 us
    convert_element_type x10, other arithmetic, shards(): keep = (keep[:half].astype(F32) + got[:half].astype(F32)).astype(BF16)  17.5 us
    pallas_call x1, Pallas kernels, self_backward(): pl.pallas_call(functools.partial(self_backward_kernel, earlier=earlier),...  11.3 us
    pallas_call x1, Pallas kernels, self_forward(): pl.pallas_call(functools.partial(self_forward_kernel, earlier=earlier), g...  9.7 us
  transfers between devices with their start and end apart: 45, of which 20 were waited for; matrix products, arithmetic and copies ran while one was open for 30% of the time, Pallas kernels for 22%

profile of v1, /device:TPU:0, one launch (start us, length us, event | category | flops | bytes accessed | tf_op | source)
XLA Modules:
  0.0 341.2 jit_solution(6568281061528970753)
XLA Ops:
  0.7 5.8 %collective-permute-start.1 = (bf16[256,1024]{1,0:T(8,128)(2,1)}, bf16[256,1024]{1,0:T(8,128)(2,1)}, u32[]{:S(2)}, u32[]{:S(2)}) collective-permute-start(bf16[256,1024]{1,0:T(8,128)(2,1)} %param.19), channel_id=1, source_target_pairs={{0,2},{1,3},{4,6},{5,7},{8,10},{9,11},{12,14},{13,15},{16,18},{17,... | collective-permute-start | bytes 1572872 | tf_op jit(solution)/shard_map/ppermute | solution.py:537
  15.5 7.2 %collective-permute-done.5 = bf16[128,1024]{1,0:T(8,128)(2,1)} collective-permute-done((bf16[128,1024]{1,0:T(8,128)(2,1)S(1)}, bf16[128,1024]{1,0:T(8,128)(2,1)}, u32[]{:S(2)}, u32[]{:S(2)}) %collective-permute-start.5) | collective-permute-done | bytes 262176 | tf_op jit(solution)/shard_map/ppermute | solution.py:542
  28.2 4.3 %fusion.23 = (bf16[512,1024]{1,0:T(8,128)(2,1)S(1)}, bf16[512,1024]{1,0:T(8,128)(2,1)S(1)}) fusion(f32[512]{0:T(512)S(1)} %add_rsqrt_fusion.2, f32[1024]{0:T(1024)S(1)} %convert_element_type.676, bf16[256,1024]{1,0:T(8,128)(2,1)} %collective-permute-done.1, bf16[256,1024]{1,0:T(8,128)(2,1)S(1)} %collective-permute-done.2, pred[]{:T(512)S(6)} %eq.59, ...), kind=kLoop, calls=%fused_computation.37 | loop fusion | flops 13631488 | bytes 4202497 | tf_op jit(solution)/shard_map/convert_element_type | solution.py:485
  39.0 9.7 %self_forward.1 = (bf16[512,512]{1,0:T(8,128)(2,1)}, f32[2,8,512]{2,1,0:T(8,128)}) custom-call(s32[1]{0:T(128)} %bitcast.1.valid_ref, f32[2,8,256]{2,1,0:T(8,128)} %pad.4.table_ref, bf16[512,512]{1,0:T(8,128)(2,1)} %convolution_convert_fusion.4.q_ref, bf16[512,256]{1,0:T(8,128)(2,1)} %convolution_convert_fusion.8.k_ref, ...), custom_call_target="tpu_custom_call" | custom-call | tf_op jit(solution)/shard_map/self_forward/pallas_call | solution.py:126
  55.5 7.5 %cross_forward.1 = (bf16[512,512]{1,0:T(8,128)(2,1)}, f32[2,8,512]{2,1,0:T(8,128)}) custom-call(bf16[512,512]{1,0:T(8,128)(2,1)} %convolution_convert_fusion.3.q_ref, bf16[256,256]{1,0:T(8,128)(2,1)} %convolution_convert_fusion.10.k_ref, bf16[256,256]{1,0:T(8,128)(2,1)} %convolution_convert_fusion.9.v_ref, f32[256,256]{1,0:T(8,128)} %broadcast_in_dim.25.own_ref), custom_call_target="tpu_custom_call" | custom-call | tf_op jit(solution)/shard_map/cross_forward/pallas_call | solution.py:309
  73.3 4.9 %fusion.7 = (bf16[512,1408]{1,0:T(8,128)(2,1)S(1)}, bf16[512,1408]{1,0:T(8,128)(2,1)}, bf16[512,1408]{1,0:T(8,128)(2,1)S(1)}) fusion(f32[512,1408]{1,0:T(8,128)S(1)} %fusion.19, f32[512,1408]{1,0:T(8,128)S(1)} %fusion.15, bf16[512,1024]{1,0:T(8,128)(2,1)S(1)} %maximum_select_fusion.2, bf16[2816,1024]{1,0:T(8,128)(2,1)S(1)} %bitcast.82, s32[]{:T(128)S(6)} %select_n.287), kind=kOutput, calls=%fused_computation.17 | convolution fusion | flops 1496580096 | bytes 14024708 | tf_op jit(solution)/shard_map/dot_general | solution.py:472
  84.6 6.6 %up_sums.1 = (bf16[8,64,1408]{2,1,0:T(8,128)(2,1)}, bf16[8,64,1408]{2,1,0:T(8,128)(2,1)}) custom-call(s32[2]{0:T(128)} %pad_add_fusion.place_ref, bf16[512,1024]{1,0:T(8,128)(2,1)} %copy-done.30, bf16[512,1408]{1,0:T(8,128)(2,1)} %copy-done.49), custom_call_target="tpu_custom_call" | custom-call | flops 1476395008 | bytes 5373952 | tf_op jit(solution)/shard_map/up_sums/pallas_call | solution.py:450
  91.2 11.0 %collective-permute-start.35 = (bf16[8,64,1408]{2,1,0:T(8,128)(2,1)}, bf16[8,64,1408]{2,1,0:T(8,128)(2,1)}, u32[]{:S(2)}, u32[]{:S(2)}) collective-permute-start(bf16[8,64,1408]{2,1,0:T(8,128)(2,1)} %get-tuple-element.63), channel_id=1, source_target_pairs={{0,2},{1,3},{2,0},{3,1},{4,6},{5,7},{6,4},{7,5},{8,10},{9,11},{10,... | collective-permute-start | bytes 4325384 | tf_op jit(solution)/shard_map/ppermute | solution.py:524
  102.2 6.4 %gate_sums.1 = (bf16[8,64,1408]{2,1,0:T(8,128)(2,1)}, bf16[8,64,1408]{2,1,0:T(8,128)(2,1)}) custom-call(s32[2]{0:T(128)} %pad_add_fusion.place_ref, bf16[512,1024]{1,0:T(8,128)(2,1)} %copy-done.30, bf16[512,1408]{1,0:T(8,128)(2,1)} %copy-done.48), custom_call_target="tpu_custom_call" | custom-call | flops 1476395008 | bytes 5373952 | tf_op jit(solution)/shard_map/gate_sums/pallas_call | solution.py:450
  110.0 4.0 %fusion.11 = f32[256,1024]{1,0:T(8,128)} fusion(bf16[2816,1024]{1,0:T(8,128)(2,1)} %param.37, s32[]{:T(128)S(6)} %select_n.287, bf16[512,1408]{1,0:T(8,128)(2,1)} %get-tuple-element.77.refs_0_, s32[]{:T(128)S(6)} %select_n.278), kind=kOutput, calls=%fused_computation.25 | convolution fusion | flops 738197504 | bytes 4653064 | tf_op jit(solution)/shard_map/dot_general | solution.py:27
  118.4 6.7 %cross_backward.1 = (bf16[512,512]{1,0:T(8,128)(2,1)}, bf16[256,256]{1,0:T(8,128)(2,1)}, bf16[256,256]{1,0:T(8,128)(2,1)}) custom-call(bf16[512,512]{1,0:T(8,128)(2,1)} %convolution_convert_fusion.3.q_ref, bf16[256,256]{1,0:T(8,128)(2,1)} %convolution_convert_fusion.10.k_ref, bf16[256,256]{1,0:T(8,128)(2,1)} %convolution_convert_fusion.9.v_ref, ...), custom_call_target="tpu_custom_call" | custom-call | tf_op jit(solution)/shard_map/cross_backward/pallas_call | solution.py:363
  133.1 7.0 %collective-permute-done.13 = bf16[2,64,1024]{2,1,0:T(8,128)(2,1)S(1)} collective-permute-done((bf16[2,64,1024]{2,1,0:T(8,128)(2,1)S(1)}, bf16[2,64,1024]{2,1,0:T(8,128)(2,1)S(1)}, u32[]{:S(2)}, u32[]{:S(2)}) %collective-permute-start.13) | collective-permute-done | bytes 262176 | tf_op jit(solution)/shard_map/ppermute | solution.py:653
  140.3 8.0 %down_sums.1 = (bf16[8,176,512]{2,1,0:T(8,128)(2,1)}, bf16[8,176,512]{2,1,0:T(8,128)(2,1)}) custom-call(s32[2]{0:T(128)} %pad_add_fusion.place_ref, bf16[512,1408]{1,0:T(8,128)(2,1)} %get-tuple-element.77.refs_0_, bf16[512,1408]{1,0:T(8,128)(2,1)} %collective-permute-done.7.refs_1_, bf16[512,512]{1,0:T(8,128)(2,1)} %constant_dynamic-slice_fusion.refs_2_), custom_call_target="tpu_custom_call" | custom-call | flops 1476395008 | bytes 6291456 | tf_op jit(solution)/shard_map/down_sums/pallas_call | solution.py:450
  169.5 11.1 %cross_sums.1 = (bf16[8,64,2048]{2,1,0:T(8,128)(2,1)}, bf16[8,64,2048]{2,1,0:T(8,128)(2,1)}) custom-call(s32[2]{0:T(128)} %pad_add_fusion.place_ref, bf16[512,512]{1,0:T(8,128)(2,1)} %get-tuple-element.43.o_ref.refs_0_, bf16[512,512]{1,0:T(8,128)(2,1)} %copy-done.38, bf16[512,1024]{1,0:T(8,128)(2,1)} %copy-done.29, bf16[256,1024]{1,0:T(8,128)(2,1)} %copy-done.8, ...), custom_call_target="tpu_custom_call" | custom-call | flops 2147483648 | bytes 9699328 | tf_op jit(solution)/shard_map/cross_sums/pallas_call | solution.py:450
  182.1 11.3 %self_backward.1 = (bf16[512,512]{1,0:T(8,128)(2,1)}, bf16[512,256]{1,0:T(8,128)(2,1)}, bf16[512,256]{1,0:T(8,128)(2,1)}, bf16[1,512,256]{2,1,0:T(8,128)(2,1)}, ...) custom-call(s32[1]{0:T(128)} %bitcast.1.valid_ref, f32[2,8,256]{2,1,0:T(8,128)} %pad.4.table_ref, ...), custom_call_target="tpu_custom_call" | custom-call | tf_op jit(solution)/shard_map/self_backward/pallas_call | solution.py:250
  198.2 8.6 %self_sums.1 = (bf16[8,64,1024]{2,1,0:T(8,128)(2,1)}, bf16[8,64,1024]{2,1,0:T(8,128)(2,1)}) custom-call(s32[2]{0:T(128)} %pad_add_fusion.place_ref, bf16[512,1024]{1,0:T(8,128)(2,1)} %copy-done.24, bf16[512,1024]{1,0:T(8,128)(2,1)} %copy-done.23, bf16[512,512]{1,0:T(8,128)(2,1)} %get-tuple-element.47.refs_2_, bf16[512,256]{1,0:T(8,128)(2,1)} %get-tuple-element.48.refs_3_, ...), custom_call_target="tpu_custom_call" | custom-call | flops 1610612736 | bytes 5767168 | tf_op jit(solution)/shard_map/self_sums/pallas_call | solution.py:450
  207.6 9.5 %collective-permute-done.11 = bf16[512,512]{1,0:T(8,128)(2,1)} collective-permute-done((bf16[512,512]{1,0:T(8,128)(2,1)}, bf16[512,512]{1,0:T(8,128)(2,1)}, u32[]{:S(2)}, u32[]{:S(2)}) %collective-permute-start.11) | collective-permute-done | bytes 524320 | tf_op jit(solution)/shard_map/ppermute | solution.py:681
  227.9 7.9 %collective-permute-done.37 = bf16[2,64,1408]{2,1,0:T(8,128)(2,1)} collective-permute-done((bf16[2,64,1408]{2,1,0:T(8,128)(2,1)}, bf16[2,64,1408]{2,1,0:T(8,128)(2,1)}, u32[]{:S(2)}, u32[]{:S(2)}) %collective-permute-start.37) | collective-permute-done | bytes 360480 | tf_op jit(solution)/shard_map/ppermute | solution.py:524
  266.2 6.5 %collective-permute-done.21 = bf16[4,64,1024]{2,1,0:T(8,128)(2,1)S(1)} collective-permute-done((bf16[4,64,1024]{2,1,0:T(8,128)(2,1)S(1)}, bf16[4,64,1024]{2,1,0:T(8,128)(2,1)S(1)}, u32[]{:S(2)}, u32[]{:S(2)}) %collective-permute-start.21) | collective-permute-done | bytes 524320 | tf_op jit(solution)/shard_map/ppermute | solution.py:524
  276.9 5.2 %collective-permute-done.22 = bf16[2,64,1024]{2,1,0:T(8,128)(2,1)S(1)} collective-permute-done((bf16[2,64,1024]{2,1,0:T(8,128)(2,1)S(1)}, bf16[2,64,1024]{2,1,0:T(8,128)(2,1)S(1)}, u32[]{:S(2)}, u32[]{:S(2)}) %collective-permute-start.22) | collective-permute-done | bytes 262176 | tf_op jit(solution)/shard_map/ppermute | solution.py:524
  289.2 7.0 %collective-permute-done.41 = bf16[4,176,512]{2,1,0:T(8,128)(2,1)S(1)} collective-permute-done((bf16[4,176,512]{2,1,0:T(8,128)(2,1)S(1)}, bf16[4,176,512]{2,1,0:T(8,128)(2,1)S(1)}, u32[]{:S(2)}, u32[]{:S(2)}) %collective-permute-start.41) | collective-permute-done | bytes 720928 | tf_op jit(solution)/shard_map/ppermute | solution.py:524
  297.9 13.6 %collective-permute-done.26 = bf16[4,64,2048]{2,1,0:T(8,128)(2,1)S(1)} collective-permute-done((bf16[4,64,2048]{2,1,0:T(8,128)(2,1)S(1)}, bf16[4,64,2048]{2,1,0:T(8,128)(2,1)S(1)}, u32[]{:S(2)}, u32[]{:S(2)}) %collective-permute-start.26) | collective-permute-done | bytes 1048608 | tf_op jit(solution)/shard_map/ppermute | solution.py:524
  319.0 10.4 %collective-permute-done.43 = bf16[1,176,512]{2,1,0:T(8,128)(2,1)S(1)} collective-permute-done((bf16[1,176,512]{2,1,0:T(8,128)(2,1)S(1)}, bf16[1,176,512]{2,1,0:T(8,128)(2,1)S(1)}, u32[]{:S(2)}, u32[]{:S(2)}) %collective-permute-start.43) | collective-permute-done | bytes 180256 | tf_op jit(solution)/shard_map/ppermute | solution.py:524
  332.3 5.0 %collective-permute-done.28 = bf16[1,64,2048]{2,1,0:T(8,128)(2,1)S(1)} collective-permute-done((bf16[1,64,2048]{2,1,0:T(8,128)(2,1)S(1)}, bf16[1,64,2048]{2,1,0:T(8,128)(2,1)S(1)}, u32[]{:S(2)}, u32[]{:S(2)}) %collective-permute-start.28) | collective-permute-done | bytes 262176 | tf_op jit(solution)/shard_map/ppermute | solution.py:524
  (355 shorter events, 153.3 us)
Async XLA Ops:
  0.7 23.2 %collective-permute-start.1 = (bf16[256,1024]{1,0:T(8,128)(2,1)}, bf16[256,1024]{1,0:T(8,128)(2,1)}, u32[]{:S(2)}, u32[]{:S(2)}) collective-permute-start(bf16[256,1024]{1,0:T(8,128)(2,1)} %param.19), channel_id=1, source_target_pairs={{0,2},{1,3},{4,6},{5,7},{8,10},{9,11},{12,14},{13,15},{16,18},{17,... | collective-permute-start | bytes 1572872 | tf_op jit(solution)/shard_map/ppermute | solution.py:537
  6.5 19.6 %collective-permute-start = (bf16[256,1024]{1,0:T(8,128)(2,1)}, bf16[256,1024]{1,0:T(8,128)(2,1)S(1)}, u32[]{:S(2)}, u32[]{:S(2)}) collective-permute-start(bf16[256,1024]{1,0:T(8,128)(2,1)} %param.19), channel_id=1, source_target_pairs={{0,1},{1,0},{2,3},{3,2},{4,5},{5,4},{6,7},{7,6},{8,9},{9,8},{10,11... | collective-permute-start | bytes 1572872 | tf_op jit(solution)/shard_map/ppermute | solution.py:521
  7.0 56.1 %collective-permute-start.8 = (bf16[256,1024]{1,0:T(8,128)(2,1)}, bf16[256,1024]{1,0:T(8,128)(2,1)}, u32[]{:S(2)}, u32[]{:S(2)}) collective-permute-start(bf16[256,1024]{1,0:T(8,128)(2,1)} %param.21), channel_id=1, source_target_pairs={{0,1},{1,0},{2,3},{3,2},{4,5},{5,4},{6,7},{7,6},{8,9},{9,8},{10,11... | collective-permute-start | bytes 1572872 | tf_op jit(solution)/shard_map/ppermute | solution.py:521
  81.9 32.1 %collective-permute-start.9 = (bf16[512,1024]{1,0:T(8,128)(2,1)S(1)}, bf16[512,1024]{1,0:T(8,128)(2,1)S(1)}, u32[]{:S(2)}, u32[]{:S(2)}) collective-permute-start(bf16[512,1024]{1,0:T(8,128)(2,1)S(1)} %add_convert_fusion.2), channel_id=1, source_target_pairs={{0,1},{1,0},{2,3},{3,2},{4,5},{5,4},{6,7},{7,6},{8,9},{9,8},{10,11... | collective-permute-start | bytes 3145736 | tf_op jit(solution)/shard_map/ppermute | solution.py:521
  84.5 55.8 %collective-permute-start.7 = (bf16[512,1408]{1,0:T(8,128)(2,1)}, bf16[512,1408]{1,0:T(8,128)(2,1)}, u32[]{:S(2)}, u32[]{:S(2)}) collective-permute-start(bf16[512,1408]{1,0:T(8,128)(2,1)} %get-tuple-element.77.refs_0_), channel_id=1, source_target_pairs={{0,1},{1,0},{2,3},{3,2},{4,5},{5,4},{6,7},{7,6},{8,9},{9,8},{10,11... | collective-permute-start | bytes 4325384 | tf_op jit(solution)/shard_map/ppermute | solution.py:521
  91.2 58.7 %collective-permute-start.35 = (bf16[8,64,1408]{2,1,0:T(8,128)(2,1)}, bf16[8,64,1408]{2,1,0:T(8,128)(2,1)}, u32[]{:S(2)}, u32[]{:S(2)}) collective-permute-start(bf16[8,64,1408]{2,1,0:T(8,128)(2,1)} %get-tuple-element.63), channel_id=1, source_target_pairs={{0,2},{1,3},{2,0},{3,1},{4,6},{5,7},{6,4},{7,5},{8,10},{9,11},{10,... | collective-permute-start | bytes 4325384 | tf_op jit(solution)/shard_map/ppermute | solution.py:524
  108.6 44.9 %collective-permute-start.30 = (bf16[8,64,1408]{2,1,0:T(8,128)(2,1)}, bf16[8,64,1408]{2,1,0:T(8,128)(2,1)}, u32[]{:S(2)}, u32[]{:S(2)}) collective-permute-start(bf16[8,64,1408]{2,1,0:T(8,128)(2,1)} %get-tuple-element.61), channel_id=1, source_target_pairs={{0,4},{1,5},{2,6},{3,7},{4,0},{5,1},{6,2},{7,3},{8,12},{9,13},{10,... | collective-permute-start | bytes 4325384 | tf_op jit(solution)/shard_map/ppermute | solution.py:524
  125.1 37.8 %collective-permute-start.10 = (bf16[512,512]{1,0:T(8,128)(2,1)}, bf16[512,512]{1,0:T(8,128)(2,1)}, u32[]{:S(2)}, u32[]{:S(2)}) collective-permute-start(bf16[512,512]{1,0:T(8,128)(2,1)} %get-tuple-element.45.refs_7_), channel_id=1, source_target_pairs={{0,1},{1,0},{2,3},{3,2},{4,5},{5,4},{6,7},{7,6},{8,9},{9,8},{10,11... | collective-permute-start | bytes 1572872 | tf_op jit(solution)/shard_map/ppermute | solution.py:521
  140.2 17.9 %collective-permute-start.14 = (bf16[1,64,1024]{2,1,0:T(8,128)(2,1)S(1)}, bf16[1,64,1024]{2,1,0:T(8,128)(2,1)S(1)}, u32[]{:S(2)}, u32[]{:S(2)}) collective-permute-start(bf16[1,64,1024]{2,1,0:T(8,128)(2,1)S(1)} %slice.422), channel_id=1, source_target_pairs={{0,1},{1,0},{2,3},{3,2},{4,5},{5,4},{6,7},{7,6},{8,9},{9,8},{10,11... | collective-permute-start | bytes 393224 | tf_op jit(solution)/shard_map/ppermute | solution.py:653
  148.3 126.1 %collective-permute-start.40 = (bf16[8,176,512]{2,1,0:T(8,128)(2,1)}, bf16[8,176,512]{2,1,0:T(8,128)(2,1)}, u32[]{:S(2)}, u32[]{:S(2)}) collective-permute-start(bf16[8,176,512]{2,1,0:T(8,128)(2,1)} %get-tuple-element.65), channel_id=1, source_target_pairs={{0,8},{1,9},{2,10},{3,11},{4,12},{5,13},{6,14},{7,15},{8,0},{9,1},... | collective-permute-start | bytes 4325384 | tf_op jit(solution)/shard_map/ppermute | solution.py:524
  153.0 66.5 %collective-permute-start.36 = (bf16[4,64,1408]{2,1,0:T(8,128)(2,1)}, bf16[4,64,1408]{2,1,0:T(8,128)(2,1)}, u32[]{:S(2)}, u32[]{:S(2)}) collective-permute-start(bf16[4,64,1408]{2,1,0:T(8,128)(2,1)} %get-tuple-element.84), channel_id=1, source_target_pairs={{0,8},{1,9},{2,10},{3,11},{4,12},{5,13},{6,14},{7,15},{8,0},{9,1},... | collective-permute-start | bytes 2162696 | tf_op jit(solution)/shard_map/ppermute | solution.py:524
  156.4 66.1 %collective-permute-start.31 = (bf16[4,64,1408]{2,1,0:T(8,128)(2,1)}, bf16[4,64,1408]{2,1,0:T(8,128)(2,1)}, u32[]{:S(2)}, u32[]{:S(2)}) collective-permute-start(bf16[4,64,1408]{2,1,0:T(8,128)(2,1)} %get-tuple-element.86), channel_id=1, source_target_pairs={{0,2},{1,3},{2,0},{3,1},{4,6},{5,7},{6,4},{7,5},{8,10},{9,11},{10,... | collective-permute-start | bytes 2162696 | tf_op jit(solution)/shard_map/ppermute | solution.py:524
  180.6 102.4 %collective-permute-start.25 = (bf16[8,64,2048]{2,1,0:T(8,128)(2,1)}, bf16[8,64,2048]{2,1,0:T(8,128)(2,1)}, u32[]{:S(2)}, u32[]{:S(2)}) collective-permute-start(bf16[8,64,2048]{2,1,0:T(8,128)(2,1)} %get-tuple-element.59), channel_id=1, source_target_pairs={{0,4},{1,5},{2,6},{3,7},{4,0},{5,1},{6,2},{7,3},{8,12},{9,13},{10,... | collective-permute-start | bytes 6291464 | tf_op jit(solution)/shard_map/ppermute | solution.py:524
  196.2 21.0 %collective-permute-start.11 = (bf16[512,512]{1,0:T(8,128)(2,1)}, bf16[512,512]{1,0:T(8,128)(2,1)}, u32[]{:S(2)}, u32[]{:S(2)}) collective-permute-start(bf16[512,512]{1,0:T(8,128)(2,1)} %pad_maximum_fusion), channel_id=1, source_target_pairs={{2,0},{3,1},{6,4},{7,5},{10,8},{11,9},{14,12},{15,13},{18,16},{19,... | collective-permute-start | bytes 1572872 | tf_op jit(solution)/shard_map/ppermute | solution.py:681
  217.2 38.9 %collective-permute-start.20 = (bf16[8,64,1024]{2,1,0:T(8,128)(2,1)}, bf16[8,64,1024]{2,1,0:T(8,128)(2,1)}, u32[]{:S(2)}, u32[]{:S(2)}) collective-permute-start(bf16[8,64,1024]{2,1,0:T(8,128)(2,1)} %get-tuple-element.57), channel_id=1, source_target_pairs={{0,2},{1,3},{2,0},{3,1},{4,6},{5,7},{6,4},{7,5},{8,10},{9,11},{10,... | collective-permute-start | bytes 3145736 | tf_op jit(solution)/shard_map/ppermute | solution.py:524
  222.5 13.3 %collective-permute-start.37 = (bf16[2,64,1408]{2,1,0:T(8,128)(2,1)}, bf16[2,64,1408]{2,1,0:T(8,128)(2,1)}, u32[]{:S(2)}, u32[]{:S(2)}) collective-permute-start(bf16[2,64,1408]{2,1,0:T(8,128)(2,1)} %get-tuple-element.94), channel_id=1, source_target_pairs={{0,4},{1,5},{2,6},{3,7},{4,0},{5,1},{6,2},{7,3},{8,12},{9,13},{10,... | collective-permute-start | bytes 1081352 | tf_op jit(solution)/shard_map/ppermute | solution.py:524
  225.1 17.9 %collective-permute-start.32 = (bf16[2,64,1408]{2,1,0:T(8,128)(2,1)}, bf16[2,64,1408]{2,1,0:T(8,128)(2,1)}, u32[]{:S(2)}, u32[]{:S(2)}) collective-permute-start(bf16[2,64,1408]{2,1,0:T(8,128)(2,1)} %get-tuple-element.96), channel_id=1, source_target_pairs={{0,8},{1,9},{2,10},{3,11},{4,12},{5,13},{6,14},{7,15},{8,0},{9,1},... | collective-permute-start | bytes 1081352 | tf_op jit(solution)/shard_map/ppermute | solution.py:524
  240.4 19.2 %collective-permute-start.38 = (bf16[1,64,1408]{2,1,0:T(8,128)(2,1)S(1)}, bf16[1,64,1408]{2,1,0:T(8,128)(2,1)S(1)}, u32[]{:S(2)}, u32[]{:S(2)}) collective-permute-start(bf16[1,64,1408]{2,1,0:T(8,128)(2,1)S(1)} %add_convert_fusion.27), channel_id=1, source_target_pairs={{0,16},{1,17},{2,18},{3,19},{4,20},{5,21},{6,22},{7,23},{8,24},{9,... | collective-permute-start | bytes 540680 | tf_op jit(solution)/shard_map/ppermute | solution.py:524
  257.7 14.9 %collective-permute-start.21 = (bf16[4,64,1024]{2,1,0:T(8,128)(2,1)S(1)}, bf16[4,64,1024]{2,1,0:T(8,128)(2,1)S(1)}, u32[]{:S(2)}, u32[]{:S(2)}) collective-permute-start(bf16[4,64,1024]{2,1,0:T(8,128)(2,1)S(1)} %get-tuple-element.90), channel_id=1, source_target_pairs={{0,8},{1,9},{2,10},{3,11},{4,12},{5,13},{6,14},{7,15},{8,0},{9,1},... | collective-permute-start | bytes 1572872 | tf_op jit(solution)/shard_map/ppermute | solution.py:524
  276.3 20.0 %collective-permute-start.41 = (bf16[4,176,512]{2,1,0:T(8,128)(2,1)S(1)}, bf16[4,176,512]{2,1,0:T(8,128)(2,1)S(1)}, u32[]{:S(2)}, u32[]{:S(2)}) collective-permute-start(bf16[4,176,512]{2,1,0:T(8,128)(2,1)S(1)} %get-tuple-element.82), channel_id=1, source_target_pairs={{0,4},{1,5},{2,6},{3,7},{4,0},{5,1},{6,2},{7,3},{8,12},{9,13},{10,... | collective-permute-start | bytes 2162696 | tf_op jit(solution)/shard_map/ppermute | solution.py:524
  285.3 26.2 %collective-permute-start.26 = (bf16[4,64,2048]{2,1,0:T(8,128)(2,1)S(1)}, bf16[4,64,2048]{2,1,0:T(8,128)(2,1)S(1)}, u32[]{:S(2)}, u32[]{:S(2)}) collective-permute-start(bf16[4,64,2048]{2,1,0:T(8,128)(2,1)S(1)} %get-tuple-element.80), channel_id=1, source_target_pairs={{0,2},{1,3},{2,0},{3,1},{4,6},{5,7},{6,4},{7,5},{8,10},{9,11},{10,... | collective-permute-start | bytes 3145736 | tf_op jit(solution)/shard_map/ppermute | solution.py:524
  296.5 19.3 %collective-permute-start.42 = (bf16[2,176,512]{2,1,0:T(8,128)(2,1)S(1)}, bf16[2,176,512]{2,1,0:T(8,128)(2,1)S(1)}, u32[]{:S(2)}, u32[]{:S(2)}) collective-permute-start(bf16[2,176,512]{2,1,0:T(8,128)(2,1)S(1)} %get-tuple-element.92), channel_id=1, source_target_pairs={{0,2},{1,3},{2,0},{3,1},{4,6},{5,7},{6,4},{7,5},{8,10},{9,11},{10,... | collective-permute-start | bytes 1081352 | tf_op jit(solution)/shard_map/ppermute | solution.py:524
  311.9 17.7 %collective-permute-start.27 = (bf16[2,64,2048]{2,1,0:T(8,128)(2,1)S(1)}, bf16[2,64,2048]{2,1,0:T(8,128)(2,1)S(1)}, u32[]{:S(2)}, u32[]{:S(2)}) collective-permute-start(bf16[2,64,2048]{2,1,0:T(8,128)(2,1)S(1)} %get-tuple-element.88), channel_id=1, source_target_pairs={{0,8},{1,9},{2,10},{3,11},{4,12},{5,13},{6,14},{7,15},{8,0},{9,1},... | collective-permute-start | bytes 1572872 | tf_op jit(solution)/shard_map/ppermute | solution.py:524
  315.8 13.7 %collective-permute-start.43 = (bf16[1,176,512]{2,1,0:T(8,128)(2,1)S(1)}, bf16[1,176,512]{2,1,0:T(8,128)(2,1)S(1)}, u32[]{:S(2)}, u32[]{:S(2)}) collective-permute-start(bf16[1,176,512]{2,1,0:T(8,128)(2,1)S(1)} %add_convert_fusion.25), channel_id=1, source_target_pairs={{0,16},{1,17},{2,18},{3,19},{4,20},{5,21},{6,22},{7,23},{8,24},{9,... | collective-permute-start | bytes 540680 | tf_op jit(solution)/shard_map/ppermute | solution.py:524
  (77 other events, 541.5 us)
